TPU v7x, 32 devices: a whole 2x2x4 slice. The times are simulated.
32 devices in a mesh: inp: 4 (over x, core), chan: 8 (over z, y).
Axes of the slice: x: 2, y: 2, z: 4, core: 2. Of those that a mesh axis runs over, the one named last changes fastest.
Arguments:
- voltages: bfloat16 [1024, 262144], P('inp', 'chan'), may hold values from -4 to 4
- scale_codes: int32 [1024], P('inp'), may hold values from 4 to 32
- kept_channels: int32 [128], replicated, may hold values from 0 to 4095, as said below
Outputs:
- visibilities: float32 [2, 128, 1024, 1024], P(None, 'chan', 'inp')
Inputs may be any that keep to these rules, and one draw needn't show every extreme that they name: `kept_channels`: 128 distinct channel numbers.
All inputs are finite; a program needn't handle non-finite values.
Results may differ from a plain program's by a relative error of at most 0.0036.
Values may be sent and summed in bfloat16 or wider, within the bound.
No kernel may reach another device: no remote copies, remote signals or barrier semaphores. Data moves between devices by JAX's collectives and lax.ppermute only.
A program may use at most 384 MiB of HBM per device.

v0:
```python
import jax
import jax.numpy as jnp
from jax import lax
from jax.sharding import PartitionSpec as P

TRANSFORM = 8192
TAPS = 4


def shifted(block, axis, distance):
    devices = range(lax.axis_size(axis))
    route = [(i - distance, i) for i in devices if i - distance in devices]
    return lax.ppermute(block, axis, route)


def prototype():
    sample = jnp.arange(TAPS * TRANSFORM, dtype=jnp.float32)
    offset = (sample + 0.5) / TRANSFORM - TAPS / 2.0
    window = 0.5 - 0.5 * jnp.cos(2.0 * jnp.pi * (sample + 0.5) / (TAPS * TRANSFORM))
    return (jnp.sinc(offset) * window).reshape(TAPS, TRANSFORM)


def dft_table(kept_channels):
    sample = jnp.arange(TRANSFORM, dtype=jnp.int32)
    phase_int = kept_channels[None, :] * sample[:, None] % TRANSFORM
    angles = phase_int.astype(jnp.float32) * (2.0 * jnp.pi / TRANSFORM)
    norming = 1.0 / jnp.sqrt(jnp.float32(TRANSFORM))
    return jnp.stack([jnp.cos(angles), -jnp.sin(angles)], axis=-1) * norming


def transform(filtered, transform_table):
    return jnp.einsum(
        "isn,nkp->kspi",
        filtered,
        transform_table,
        precision=lax.Precision.HIGHEST,
        preferred_element_type=jnp.float32,
    )


def local(voltages, scale_codes, kept_channels):
    in_rows = voltages.shape[0]
    spec_dev = voltages.shape[1] // TRANSFORM
    history = TAPS - 1
    frames = voltages.reshape(in_rows, spec_dev, TRANSFORM)
    coeffs = prototype()
    transform_table = dft_table(kept_channels)
    filtered = sum(
        (
            jnp.pad(
                coeffs[tap_index][None, None, :] * frames.astype(jnp.float32),
                ((0, 0), (history - tap_index, tap_index), (0, 0)),
            )
            for tap_index in range(TAPS)
        )
    )
    result = transform(filtered, transform_table)
    incoming = shifted(result[:, spec_dev:], "chan", 1)
    spectra = result[:, :spec_dev] + jnp.pad(
        incoming, ((0, 0), (0, spec_dev - history), (0, 0), (0, 0))
    )
    scales = scale_codes.astype(jnp.float32) / 16.0
    channelized = (
        (spectra * scales).astype(jnp.bfloat16).reshape(spectra.shape[0], spec_dev * 2, in_rows)
    )
    turned = lax.all_to_all(channelized, "chan", split_axis=0, concat_axis=1, tiled=True)
    spectra_count = turned.shape[1] // 2
    columns = lax.all_gather(turned, "inp", axis=2, tiled=True)
    halves = columns.reshape(columns.shape[0], spectra_count, 2, columns.shape[2])
    rotated = jnp.stack([-halves[:, :, 1], halves[:, :, 0]], axis=2).reshape(columns.shape)
    real_part = jnp.einsum("kja,kjb->kab", turned, columns, preferred_element_type=jnp.float32)
    imag_part = jnp.einsum("kja,kjb->kab", turned, rotated, preferred_element_type=jnp.float32)
    return jnp.stack([real_part, imag_part]) / spectra_count


def solution(mesh):
    placed = (P("inp", "chan"), P("inp"), P())
    return jax.shard_map(
        local, mesh=mesh, in_specs=placed, out_specs=P(None, "chan", "inp", None), check_vma=False
    )
```

profile of v0, /device:TPU:0, one launch (start us, length us, event | category | flops | bytes accessed | tf_op | source)
XLA Modules:
  0.0 263.1 jit_solution(11211198881875391109)
XLA Ops:
  6.5 0.6 fusion.32
  7.2 0.0 copy-start.1
  7.2 18.3 %convert_element_type.49 = f32[256,32768]{1,0:T(8,128)} convert(bf16[256,32768]{1,0:T(8,128)(2,1)} %param.3) | non-fusion elementwise | flops 8388608 | bytes 50331648 | tf_op jit(solution)/shard_map/convert_element_type | solution.py:51
  25.5 0.0 copy-done.1
  25.5 19.0 %fusion.20 = (f32[8192,128,1]{0,1,2:T(8,128)}, f32[8192,128,1]{0,1,2:T(8,128)}) fusion(s32[128]{0:T(128)S(1)} %copy-done.1), kind=kLoop, calls=%fused_computation.33 | loop fusion | flops 15728640 | bytes 8389120 | tf_op jit(solution)/shard_map/cos | solution.py:28
  44.5 54.6 %bitcast_multiply_fusion.3 = (f32[256,4,8192]{2,0,1:T(8,128)}, f32[256,4,8192]{2,0,1:T(8,128)}, f32[256,4,8192]{2,0,1:T(8,128)}, f32[256,4,8192]{2,0,1:T(8,128)}) fusion(f32[32,4,8,8192]{3,2,1,0:T(8,128)} %bitcast.43, f32[8192]{0:T(1024)S(1)} %get-tuple-element.11, f32[8192]{0:T(1024)S(1)} %get-tuple-element.12, f32[8192]{0:T(1024)S(1)} %get-tuple-element.13, ...), kind=kLoop, calls=%fused_computation.12 | loop fusion | flops 33554432 | bytes 167903232 | tf_op jit(solution)/shard_map/mul | solution.py:51
  99.1 58.1 %fusion.21 = f32[128,7,2,256]{3,0,1,2:T(8,128)S(1)} fusion(f32[256,4,8192]{2,0,1:T(8,128)} %get-tuple-element.6, f32[256,4,8192]{2,0,1:T(8,128)} %get-tuple-element.7, f32[256,4,8192]{2,0,1:T(8,128)} %get-tuple-element.8, f32[256,4,8192]{2,0,1:T(8,128)} %get-tuple-element.5, f32[8192,128,1]{0,1,2:T(8,128)} %get-tuple-element.16, ...), kind=kOutput, calls=%fused_computation.34 | convolution fusion | flops 45145391104 | bytes 144441344 | tf_op jit(solution)/shard_map/isn,nkp->kspi/dot_general | solution.py:32
  157.2 0.1 slice.41
  157.3 4.9 %collective-permute-start = (f32[128,3,2,256]{3,0,1,2:T(8,128)S(1)}, f32[128,3,2,256]{3,0,1,2:T(8,128)S(1)}, u32[]{:S(2)}, u32[]{:S(2)}) collective-permute-start(f32[128,3,2,256]{3,0,1,2:T(8,128)S(1)} %slice.41), channel_id=1, source_target_pairs={{0,1},{1,2},{2,3},{3,4},{4,5},{5,6},{6,7},{8,9},{9,10},{10,11},{11... | collective-permute-start | bytes 2359304 | tf_op jit(solution)/shard_map/ppermute | solution.py:13
  162.2 0.0 copy-done
  162.3 16.7 %collective-permute-done = f32[128,3,2,256]{3,0,1,2:T(8,128)S(1)} collective-permute-done((f32[128,3,2,256]{3,0,1,2:T(8,128)S(1)}, f32[128,3,2,256]{3,0,1,2:T(8,128)S(1)}, u32[]{:S(2)}, u32[]{:S(2)}) %collective-permute-start) | collective-permute-done | bytes 786464 | tf_op jit(solution)/shard_map/ppermute | solution.py:13
  179.0 0.1 fusion.27
  179.2 0.3 copy.20
  179.5 20.2 %all_to_all.18 = bf16[128,8,256]{2,1,0:T(8,128)(2,1)S(1)} all-to-all(bf16[128,8,256]{2,1,0:T(8,128)(2,1)S(1)} %copy.20), channel_id=1, replica_groups=mesh['inp'=4,'chan'=8] {'chan'}, dimensions={0} | all-to-all | bytes 1048576 | tf_op jit(solution)/shard_map/all_to_all | solution.py:66
  199.6 0.8 copy.31
  200.5 0.0 all-gather.2.cloned.1.call-update
  200.5 22.1 %all-gather.2.cloned.1.call-done = bf16[16,64,1024]{2,1,0:T(8,128)(2,1)} async-done(((bf16[16,64,256]{2,1,0:T(8,128)(2,1)}), bf16[16,64,1024]{2,1,0:T(8,128)(2,1)}) %all-gather.2.cloned.1.call-update) | async-done | bytes 2097168 | tf_op jit(solution)/shard_map/all_gather | solution.py:68
  222.6 2.7 %reshape.123 = bf16[16,32,2,1024]{3,2,1,0:T(2,128)(2,1)S(1)} reshape(bf16[16,64,1024]{2,1,0:T(8,128)(2,1)} %all-gather.2.cloned.1.call-done) | data formatting | bytes 4194304 | tf_op jit(solution)/shard_map/reshape | solution.py:69
  225.3 4.7 %slice_negate_fusion = (bf16[16,32,1,1024]{3,2,1,0:T(2,128)(2,1)S(1)}, bf16[16,32,1,1024]{3,2,1,0:T(2,128)(2,1)S(1)}) fusion(bf16[16,32,2,1024]{3,2,1,0:T(2,128)(2,1)S(1)} %reshape.123), kind=kLoop, calls=%fused_computation.31 | loop fusion | flops 524288 | bytes 4194304 | tf_op jit(solution)/shard_map/neg | solution.py:70
  230.0 4.4 %pad_maximum_fusion = bf16[16,32,2,1024]{3,2,1,0:T(2,128)(2,1)S(1)} fusion(bf16[16,32,1,1024]{3,2,1,0:T(2,128)(2,1)S(1)} %get-tuple-element.10, bf16[16,32,1,1024]{3,2,1,0:T(2,128)(2,1)S(1)} %get-tuple-element.9), kind=kLoop, calls=%fused_computation.32 | loop fusion | flops 4194304 | bytes 4194304 | tf_op jit(solution)/shard_map/stack | solution.py:70
  234.4 2.2 reshape.124
  236.6 4.0 %convolution_bitcast_fusion = f32[1,16,256,1024]{3,2,1,0:T(8,128)S(1)} fusion(bf16[16,64,1024]{2,1,0:T(8,128)(2,1)} %reshape.124, bf16[16,8,8,256]{3,2,0,1:T(8,128)(2,1)S(1)} %bitcast.45), kind=kOutput, calls=%fused_computation.14 | convolution fusion | flops 536870912 | bytes 19398656 | tf_op jit(solution)/shard_map/kja,kjb->kab/dot_general | solution.py:72
  240.6 4.0 %convolution_bitcast_fusion.1 = f32[1,16,256,1024]{3,2,1,0:T(8,128)S(1)} fusion(bf16[16,64,1024]{2,1,0:T(8,128)(2,1)} %all-gather.2.cloned.1.call-done, bf16[16,8,8,256]{3,2,0,1:T(8,128)(2,1)S(1)} %bitcast.46), kind=kOutput, calls=%fused_computation.15 | convolution fusion | flops 536870912 | bytes 19398656 | tf_op jit(solution)/shard_map/kja,kjb->kab/dot_general | solution.py:71
  244.6 11.7 %maximum_multiply_fusion = f32[2,16,256,1024]{3,2,1,0:T(8,128)} fusion(f32[1,16,256,1024]{3,2,1,0:T(8,128)S(1)} %convolution_bitcast_fusion, f32[1,16,256,1024]{3,2,1,0:T(8,128)S(1)} %convolution_bitcast_fusion.1), kind=kLoop, calls=%fused_computation.13 | loop fusion | flops 16777216 | bytes 67108864 | tf_op jit(solution)/shard_map/div | solution.py:73
  (5 shorter events, 0.1 us)
Async XLA Ops:
  6.5 216.0 %all-gather.2.cloned.1.call-start = ((), (), s32[]{:S(2)}) async-start(), calls=%async_computation.1 | async-start | bytes 2621440 | tf_op jit(solution)/shard_map/all_gather | solution.py:68
  7.2 18.3 %copy-start.1 = (s32[128]{0:T(128)S(1)}, s32[128]{0:T(128)}, u32[]{:S(2)}) copy-start(s32[128]{0:T(128)} %param.5) | copy-start | bytes 1540
  99.1 63.1 %copy-start = (s32[256]{0:T(256)S(1)}, s32[256]{0:T(256)}, u32[]{:S(2)}) copy-start(s32[256]{0:T(256)} %param.4) | copy-start | bytes 3076
  157.3 21.7 %collective-permute-start = (f32[128,3,2,256]{3,0,1,2:T(8,128)S(1)}, f32[128,3,2,256]{3,0,1,2:T(8,128)S(1)}, u32[]{:S(2)}, u32[]{:S(2)}) collective-permute-start(f32[128,3,2,256]{3,0,1,2:T(8,128)S(1)} %slice.41), channel_id=1, source_target_pairs={{0,1},{1,2},{2,3},{3,4},{4,5},{5,6},{6,7},{8,9},{9,10},{10,11},{11... | collective-permute-start | bytes 2359304 | tf_op jit(solution)/shard_map/ppermute | solution.py:13
Sparse Core Ops, SparseCore 0:
  200.6 21.8 all-gather.1
where the time goes:
time: 264 us; the launch traced here: 263 us
  other arithmetic  113 us (43%)
  matrix products  66.1 us (25%)
  waiting for transfers between devices  38.8 us (15%)
  blocking collectives  20.2 us (8%)
  between operations  13.5 us (5%)
  local copies, waits for them, and re-layouts  6.21 us (2%)
  starting transfers between devices  4.92 us (2%)
    dot_general x1, matrix products, transform(): jnp.einsum('isn,nkp->kspi', filtered, transform_table, precision=lax.Prec...  58.1 us
    mul x1, other arithmetic, local(): coeffs[tap_index][None, None, :] * frames.astype(jnp.float32)  54.6 us
    all_gather x1, waiting for transfers between devices, local(): columns = lax.all_gather(turned, 'inp', axis=2, tiled=True)  22.1 us
    all_to_all x1, blocking collectives, local(): lax.all_to_all(channelized, 'chan', split_axis=0, concat_axis=1, tiled=True)  20.2 us
    cos x1, other arithmetic, dft_table(): return jnp.stack([jnp.cos(angles), -jnp.sin(angles)], axis=-1) * norming  19 us
    convert_element_type x1, other arithmetic, local(): frames.astype(jnp.float32)  18.3 us
    ppermute x1, waiting for transfers between devices, shifted(): return lax.ppermute(block, axis, route)  16.7 us
    div x1, other arithmetic, local(): return jnp.stack([real_part, imag_part]) / spectra_count  11.7 us
  transfers between devices with their start and end apart: 2, of which 2 were waited for; matrix products, arithmetic and copies ran while one was open for 0% of the time, Pallas kernels for 0%

commit v1 on v0

v1 whole, which is shorter than its diff:
```python
import functools

import jax
import jax.numpy as jnp
from jax import lax
from jax.experimental import pallas as pl
from jax.experimental.pallas import tpu as pltpu
from jax.sharding import PartitionSpec as P

TRANSFORM = 8192
TAPS = 4
SUB = 128
LANES = 128
DEPTH = 1024
VMEM = 60 * 1024 * 1024


def prototype():
    sample = jnp.arange(TAPS * TRANSFORM, dtype=jnp.float32)
    offset = (sample + 0.5) / TRANSFORM - TAPS / 2.0
    window = 0.5 - 0.5 * jnp.cos(2.0 * jnp.pi * (sample + 0.5) / (TAPS * TRANSFORM))
    return (jnp.sinc(offset) * window).reshape(TAPS, TRANSFORM)


def angle_tables(kept_channels):
    coarse = jnp.arange(TRANSFORM // SUB, dtype=jnp.int32) * SUB
    fine = jnp.arange(SUB, dtype=jnp.int32)
    sample = jnp.concatenate([coarse, fine])
    turns = kept_channels[None, :] * sample[:, None] % TRANSFORM
    quarter = jnp.where(jnp.arange(sample.shape[0]) < coarse.shape[0], 0, TRANSFORM // 4)
    turns = jnp.concatenate([turns, (turns + quarter[:, None]) % TRANSFORM], axis=1)
    angles = turns.astype(jnp.float32) * (2.0 * jnp.pi / TRANSFORM)
    norming = jnp.where(quarter == 0, 1.0 / jnp.sqrt(jnp.float32(TRANSFORM)), 1.0)[:, None]
    return jnp.cos(angles) * norming, jnp.sin(angles) * norming


def dft_kernel(planes, frames, groups, *refs):
    nf = len(frames)
    samples = dict(zip(frames, refs[:nf]))
    coeff, cos_a, sin_a, cos_b, sin_b, scale = refs[nf : nf + 6]
    outs = refs[nf + 6 : nf + 6 + len(groups)]
    acc = refs[-1]
    step = pl.program_id(0)

    @pl.when(step == 0)
    def _():
        acc[...] = jnp.zeros_like(acc)

    cb, sb = cos_b[...], sin_b[...]
    table = jnp.concatenate(
        [cos_a[r : r + 1, :] * cb - sin_a[r : r + 1, :] * sb for r in range(DEPTH // SUB)], axis=0
    )
    t_hi = table.astype(jnp.bfloat16)
    t_lo = (table - t_hi.astype(jnp.float32)).astype(jnp.bfloat16)
    dot = functools.partial(jnp.dot, preferred_element_type=jnp.float32)
    volts = {f: samples[f][...].astype(jnp.float32) for f in frames}
    for p, (s, passes) in enumerate(planes):
        x = None
        for t in range(TAPS):
            f = s - (TAPS - 1) + t
            if f in volts:
                term = coeff[t : t + 1, :] * volts[f]
                x = term if x is None else x + term
        hi = x.astype(jnp.bfloat16)
        total = dot(hi, t_hi)
        if passes > 1:
            total += dot(hi, t_lo)
        if passes > 2:
            total += dot((x - hi.astype(jnp.float32)).astype(jnp.bfloat16), t_hi)
        acc[p] += total

    @pl.when(step == pl.num_programs(0) - 1)
    def _():
        for out, (members, dtype) in zip(outs, groups):
            for i, p in enumerate(members):
                out[i] = (acc[p].T * scale[...]).astype(dtype)


def spectra(voltages, coeffs, tables, scales, planes, groups):
    rows = voltages.shape[0]
    own = voltages.shape[1] // TRANSFORM
    steps = TRANSFORM // DEPTH
    columns = tables[0].shape[1]
    coarse = TRANSFORM // SUB
    frames = sorted({s - (TAPS - 1) + t for s, _ in planes for t in range(TAPS)} & set(range(own)))
    per_step = DEPTH // SUB

    def frame_spec(f):
        return pl.BlockSpec((rows, DEPTH), lambda j: (0, f * steps + j))

    coarse_spec = pl.BlockSpec((per_step, columns), lambda j: (j, 0))
    fine_spec = pl.BlockSpec((SUB, columns), lambda j: (0, 0))
    cos_t, sin_t = tables
    outs = [jax.ShapeDtypeStruct((len(m), columns, rows), d) for m, d in groups]
    flops = 2 * rows * TRANSFORM * columns * sum(p for _, p in planes)
    return pl.pallas_call(
        functools.partial(dft_kernel, planes, frames, groups),
        grid=(steps,),
        in_specs=[frame_spec(f) for f in frames]
        + [pl.BlockSpec((TAPS, DEPTH), lambda j: (0, j))]
        + [coarse_spec, coarse_spec, fine_spec, fine_spec]
        + [pl.BlockSpec((1, rows), lambda j: (0, 0))],
        out_specs=[pl.BlockSpec(o.shape, lambda j: (0, 0, 0)) for o in outs],
        out_shape=outs,
        scratch_shapes=[pltpu.VMEM((len(planes), rows, columns), jnp.float32)],
        compiler_params=pltpu.CompilerParams(vmem_limit_bytes=VMEM),
        cost_estimate=pl.CostEstimate(
            flops=flops, bytes_accessed=len(frames) * rows * TRANSFORM * 2, transcendentals=0
        ),
    )(*[voltages] * len(frames), coeffs, cos_t[:coarse], sin_t[:coarse], cos_t[coarse:], sin_t[coarse:], scales)


def combine_kernel(parts, place, own, ahead, behind, *refs):
    outs, mixed = refs[:-1], refs[-1]
    me = place[0]
    slots, columns = own.shape[0], own.shape[1]
    kept = columns // 2
    inside = jnp.where(me == parts - 1, 0.0, 1.0)
    back = behind.shape[0]
    for s in range(slots):
        value = own[s]
        if s == 0:
            value = value + ahead[0].astype(jnp.float32)
        if s >= slots - back:
            value = value * inside + behind[s - (slots - back)].astype(jnp.float32)
        for p in range(2):
            for h in range(mixed.shape[0]):
                mixed[h, pl.ds(p * slots + s, kept, stride=2 * slots), :] = value[
                    p * kept : (p + 1) * kept, h * LANES : (h + 1) * LANES
                ]
    rows = outs[0].shape[0]
    for d, out in enumerate(outs):
        start = pl.multiple_of(jnp.bitwise_xor(me, d) * rows, rows)
        for h in range(mixed.shape[0]):
            out[:, h * LANES : (h + 1) * LANES] = mixed[h, pl.ds(start, rows), :].astype(out.dtype)


def combined(parts, me, own, ahead, behind):
    slots, columns, rows = own.shape
    block = columns * slots // parts
    whole = pl.BlockSpec(memory_space=pltpu.VMEM)
    return pl.pallas_call(
        functools.partial(combine_kernel, parts),
        in_specs=[pl.BlockSpec(memory_space=pltpu.SMEM)] + [whole] * 3,
        out_specs=[whole] * parts,
        out_shape=[jax.ShapeDtypeStruct((block, rows), jnp.bfloat16)] * parts,
        scratch_shapes=[pltpu.VMEM((rows // LANES, slots * columns, LANES), jnp.float32)],
        compiler_params=pltpu.CompilerParams(vmem_limit_bytes=VMEM),
    )(me, own, ahead, behind)


def correlate_kernel(parts, half, spectra_count, place, *refs):
    mine, theirs, out = refs[:parts], refs[parts : 2 * parts], refs[-1]
    wide = 2 * half
    for c in range(mine[0].shape[0] // wide):
        take = slice(c * wide, (c + 1) * wide)
        left = jnp.concatenate([m[take].astype(jnp.float32) for m in mine], axis=0)
        right = jnp.concatenate([m[take].astype(jnp.float32) for m in theirs], axis=0).astype(jnp.bfloat16)
        count = left.shape[0]
        row = lax.broadcasted_iota(jnp.int32, left.shape, 0) % wide
        turned = jnp.where(row < half, pltpu.roll(left, count - half, 0), -pltpu.roll(left, half, 0))
        both = jnp.concatenate([left.T, turned.T], axis=0).astype(jnp.bfloat16)
        result = jnp.dot(both, right, preferred_element_type=jnp.float32) * (1.0 / spectra_count)
        out[0, c] = result[: left.shape[1]]
        out[1, c] = result[left.shape[1] :]


def correlated(column, mine, theirs, half, spectra_count, total, before=None):
    parts = len(mine)
    block, rows = mine[0].shape
    wide = 2 * half
    pair = max(1, 16 // wide)
    steps = block // (pair * wide)
    shape = jax.ShapeDtypeStruct((2, block // wide, rows, total), jnp.float32)
    spec = pl.BlockSpec((pair * wide, rows), lambda j, place: (j, 0))
    operands = [column, *mine, *theirs]
    in_specs = [spec] * (2 * parts)
    aliases = {}
    if before is not None:
        operands.append(before)
        in_specs.append(pl.BlockSpec(memory_space=pl.ANY))
        aliases = {len(operands) - 1: 0}
    return pl.pallas_call(
        functools.partial(correlate_kernel, parts, half, spectra_count),
        grid_spec=pltpu.PrefetchScalarGridSpec(
            num_scalar_prefetch=1,
            grid=(steps,),
            in_specs=in_specs,
            out_specs=pl.BlockSpec((2, pair, rows, rows), lambda j, place: (0, j, 0, place[0])),
        ),
        out_shape=shape,
        input_output_aliases=aliases,
        compiler_params=pltpu.CompilerParams(vmem_limit_bytes=VMEM),
        cost_estimate=pl.CostEstimate(
            flops=4 * spectra_count * 2 * rows * rows * 2 * block // wide,
            bytes_accessed=2 * block // wide * rows * rows * 4,
            transcendentals=0,
        ),
    )(*operands)


def exchanged(block, axis, mask):
    return lax.ppermute(block, axis, [(i, i ^ mask) for i in range(lax.axis_size(axis))])


def local(voltages, scale_codes, kept_channels):
    rows = voltages.shape[0]
    own = voltages.shape[1] // TRANSFORM
    history = TAPS - 1
    parts, groups = lax.axis_size("chan"), lax.axis_size("inp")
    me, seat = lax.axis_index("chan"), lax.axis_index("inp")
    coeffs = prototype()
    tables = angle_tables(kept_channels)
    scales = (scale_codes.astype(jnp.float32) / 16.0)[None, :]
    first = 2
    last = first + own
    edge = [(s, 1 if s in (0, own + history - 1) else 2) for s in [*range(first), *range(last, own + history)]]
    inner = [(s, 2 if s == last - 1 else 3) for s in range(first, last)]
    behind, ahead = spectra(
        voltages, coeffs, tables, scales, edge,
        [(list(range(first)), jnp.bfloat16), (list(range(first, len(edge))), jnp.bfloat16)],
    )
    ahead = lax.ppermute(ahead, "chan", [(i, i + 1) for i in range(parts - 1)])
    behind = lax.ppermute(behind, "chan", [(i, (i - 1) % parts) for i in range(parts)])
    (planes,) = spectra(voltages, coeffs, tables, scales, inner, [(list(range(own)), jnp.float32)])
    blocks = combined(parts, me[None], planes, ahead, behind)
    keep, near = blocks[0::2], [exchanged(b, "chan", 1) for b in blocks[1::2]]
    mine = [keep[0], near[0]]
    for i in range(1, parts // 2):
        mine += [exchanged(keep[i], "chan", 2 * i), exchanged(near[i], "chan", 2 * i)]
    spectra_count = own * parts
    total = rows * groups
    half = own
    across = [exchanged(m, "inp", 2) for m in mine]
    beside = [exchanged(m, "inp", 1) for m in mine]
    corner = [exchanged(m, "inp", 1) for m in across]
    result = None
    for mask, theirs in ((0, mine), (1, beside), (2, across), (3, corner)):
        column = jnp.bitwise_xor(seat, mask)[None].astype(jnp.int32)
        result = correlated(column, mine, theirs, half, spectra_count, total, result)
    return result


def solution(mesh):
    placed = (P("inp", "chan"), P("inp"), P())
    return jax.shard_map(
        local, mesh=mesh, in_specs=placed, out_specs=P(None, "chan", "inp", None), check_vma=False
    )
```

time: 264 us -> 116 us (0.44)
  other arithmetic: 113 us -> 4.78 us
  matrix products: 66.1 us -> 0 us
  Pallas kernels: 0 us -> 65.5 us
  waiting for transfers between devices: 38.8 us -> 10.2 us
  starting transfers between devices: 4.92 us -> 28.9 us
  blocking collectives: 20.2 us -> 0 us
  between operations: 13.5 us -> 0.41 us
    dot_general x3 -> x0, matrix products: 66.1 us -> none  [the longest x1 58.1 us: transform(): jnp.einsum('isn,nkp->kspi', filtered, transform_table, precision=lax.Prec...]
    pallas_call x0 -> x7, Pallas kernels: none -> 65.5 us  [the longest x2 32.2 us: spectra(): pl.pallas_call(functools.partial(dft_kernel, planes, frames, groups), gri...]
    mul x1 -> x2, other arithmetic: 54.6 us -> 0.72 us  [the longest x1 0.72 us: angle_tables(): return (jnp.cos(angles) * norming, jnp.sin(angles) * norming)]
    ppermute x1 -> x36, starting transfers between devices: 4.92 us -> 28.9 us  [the longest x34 21.6 us: exchanged(): lax.ppermute(block, axis, [(i, i ^ mask) for i in range(lax.axis_size(axi...]
    all_gather x1 -> x0, waiting for transfers between devices: 22.1 us -> none  [local(): columns = lax.all_gather(turned, 'inp', axis=2, tiled=True)]
    all_to_all x1 -> x0, blocking collectives: 20.2 us -> none  [local(): lax.all_to_all(channelized, 'chan', split_axis=0, concat_axis=1, tiled=True)]
    cos x1 -> x0, other arithmetic: 19 us -> none  [dft_table(): return jnp.stack([jnp.cos(angles), -jnp.sin(angles)], axis=-1) * norming]
    convert_element_type x2 -> x0, other arithmetic: 18.4 us -> none  [the longest x1 18.3 us: local(): frames.astype(jnp.float32)]
  transfers between devices with their start and end apart: 2 -> 36, of which waited for: 2 -> 10; matrix products, arithmetic and copies ran while one was open for 0% -> 0% of each run, Pallas kernels for 0% -> 39%
where the time goes in v1:
time: 116 us; the launch traced here: 114 us
  Pallas kernels  65.5 us (56%)
  starting transfers between devices  28.9 us (25%)
  waiting for transfers between devices  10.2 us (9%)
  other arithmetic  4.78 us (4%)
  local copies, waits for them, and re-layouts  4.03 us (3%)
    pallas_call x2, Pallas kernels, spectra(): pl.pallas_call(functools.partial(dft_kernel, planes, frames, groups), gri...  32.2 us
    pallas_call x4, Pallas kernels, correlated(): pl.pallas_call(functools.partial(correlate_kernel, parts, half, spectra_c...  30.8 us
    ppermute x34, starting transfers between devices, exchanged(): lax.ppermute(block, axis, [(i, i ^ mask) for i in range(lax.axis_size(axi...  21.6 us
    ppermute x34, waiting for transfers between devices, exchanged(): lax.ppermute(block, axis, [(i, i ^ mask) for i in range(lax.axis_size(axi...  10.2 us
    ppermute x1, starting transfers between devices, local(): lax.ppermute(behind, 'chan', [(i, (i - 1) % parts) for i in range(parts)])  6.01 us
    pallas_call x1, Pallas kernels, combined(): pl.pallas_call(functools.partial(combine_kernel, parts), in_specs=[pl.Blo...  2.45 us
  transfers between devices with their start and end apart: 36, of which 10 were waited for; matrix products, arithmetic and copies ran while one was open for 0% of the time, Pallas kernels for 39%

profile of v1, /device:TPU:0, one launch (start us, length us, event | category | flops | bytes accessed | tf_op | source)
XLA Modules:
  0.0 113.8 jit_solution(15093206282077615040)
XLA Ops:
  4.2 1.9 %fusion.6.refs_4_.refs_3_ = f32[4,8192]{1,0:T(4,128)} fusion(), kind=kLoop, calls=%fused_computation.23 | loop fusion | flops 1376256 | bytes 131072 | tf_op jit(solution)/shard_map/mul | solution.py:22
  6.1 1.3 %convert_multiply_fusion = f32[256]{0:T(256)} fusion(s32[256]{0:T(256)} %param.4), kind=kLoop, calls=%fused_computation.40 | loop fusion | flops 512 | bytes 2048 | tf_op jit(solution)/shard_map/div | solution.py:214
  7.4 11.5 %shard_map.38 = (bf16[2,256,256]{2,1,0:T(8,128)(2,1)}, bf16[1,256,256]{2,1,0:T(8,128)(2,1)}) custom-call(bf16[256,32768]{1,0:T(8,128)(2,1)} %refs_2_.3, bf16[256,32768]{1,0:T(8,128)(2,1)} %refs_2_.3, bf16[256,32768]{1,0:T(8,128)(2,1)} %refs_2_.3, f32[4,8192]{1,0:T(4,128)} %fusion.6.refs_4_.refs_3_, f32[64,256]{1,0:T(8,128)} %slice.20.refs_5_.refs_4_, ...), custom_call_target="tpu_custom_call" | custom-call | flops 4294967296 | bytes 12582912 | tf_op jit(solution)/shard_map/pallas_call | solution.py:96
  18.9 6.0 %collective-permute-start.1 = (bf16[2,256,256]{2,1,0:T(8,128)(2,1)}, bf16[2,256,256]{2,1,0:T(8,128)(2,1)S(1)}, u32[]{:S(2)}, u32[]{:S(2)}) collective-permute-start(bf16[2,256,256]{2,1,0:T(8,128)(2,1)} %get-tuple-element.16), channel_id=1, source_target_pairs={{0,7},{1,0},{2,1},{3,2},{4,3},{5,4},{6,5},{7,6},{8,15},{9,8},{10,9... | collective-permute-start | bytes 786440 | tf_op jit(solution)/shard_map/ppermute | solution.py:224
  24.9 1.3 %collective-permute-start = (bf16[1,256,256]{2,1,0:T(8,128)(2,1)}, bf16[1,256,256]{2,1,0:T(8,128)(2,1)S(1)}, u32[]{:S(2)}, u32[]{:S(2)}) collective-permute-start(bf16[1,256,256]{2,1,0:T(8,128)(2,1)} %get-tuple-element.15), channel_id=1, source_target_pairs={{0,1},{1,2},{2,3},{3,4},{4,5},{5,6},{6,7},{8,9},{9,10},{10,11},{11... | collective-permute-start | bytes 393224 | tf_op jit(solution)/shard_map/ppermute | solution.py:223
  26.2 20.7 %shard_map.37.own = f32[4,256,256]{2,1,0:T(8,128)} custom-call(bf16[256,32768]{1,0:T(8,128)(2,1)} %refs_2_.3, bf16[256,32768]{1,0:T(8,128)(2,1)} %refs_2_.3, bf16[256,32768]{1,0:T(8,128)(2,1)} %refs_2_.3, bf16[256,32768]{1,0:T(8,128)(2,1)} %refs_2_.3, f32[4,8192]{1,0:T(4,128)} %fusion.6.refs_4_.refs_3_, f32[64,256]{1,0:T(8,128)} %slice.20.refs_5_.refs_4_, ...), custom_call_target="tpu_custom_call" | custom-call | flops 11811160064 | bytes 16777216 | tf_op jit(solution)/shard_map/pallas_call | solution.py:96
  47.6 2.5 %shard_map.39 = (bf16[128,256]{1,0:T(8,128)(2,1)}, bf16[128,256]{1,0:T(8,128)(2,1)}, bf16[128,256]{1,0:T(8,128)(2,1)}, bf16[128,256]{1,0:T(8,128)(2,1)}, bf16[12...) custom-call(s32[1]{0:T(128)} %bitcast.1.place, ...), custom_call_target="tpu_custom_call" | custom-call | tf_op jit(solution)/shard_map/pallas_call | solution.py:142
  50.6 1.5 %collective-permute-start.4 = (bf16[128,256]{1,0:T(8,128)(2,1)}, bf16[128,256]{1,0:T(8,128)(2,1)S(1)}, u32[]{:S(2)}, u32[]{:S(2)}) collective-permute-start(bf16[128,256]{1,0:T(8,128)(2,1)} %get-tuple-element.20), channel_id=1, source_target_pairs={{0,1},{1,0},{2,3},{3,2},{4,5},{5,4},{6,7},{7,6},{8,9},{9,8},{10,11... | collective-permute-start | bytes 196616 | tf_op jit(solution)/shard_map/ppermute | solution.py:203
  52.6 1.5 %collective-permute-start.2 = (bf16[128,256]{1,0:T(8,128)(2,1)}, bf16[128,256]{1,0:T(8,128)(2,1)S(1)}, u32[]{:S(2)}, u32[]{:S(2)}) collective-permute-start(bf16[128,256]{1,0:T(8,128)(2,1)} %get-tuple-element.18), channel_id=1, source_target_pairs={{0,1},{1,0},{2,3},{3,2},{4,5},{5,4},{6,7},{7,6},{8,9},{9,8},{10,11... | collective-permute-start | bytes 196616 | tf_op jit(solution)/shard_map/ppermute | solution.py:203
  55.2 1.2 %collective-permute-start.6 = (bf16[128,256]{1,0:T(8,128)(2,1)}, bf16[128,256]{1,0:T(8,128)(2,1)S(1)}, u32[]{:S(2)}, u32[]{:S(2)}) collective-permute-start(bf16[128,256]{1,0:T(8,128)(2,1)} %get-tuple-element.21), channel_id=1, source_target_pairs={{0,4},{1,5},{2,6},{3,7},{4,0},{5,1},{6,2},{7,3},{8,12},{9,13},{10,... | collective-permute-start | bytes 196616 | tf_op jit(solution)/shard_map/ppermute | solution.py:203
  56.6 1.9 %collective-permute-start.9 = (bf16[128,256]{1,0:T(8,128)(2,1)}, bf16[128,256]{1,0:T(8,128)(2,1)S(1)}, u32[]{:S(2)}, u32[]{:S(2)}) collective-permute-start(bf16[128,256]{1,0:T(8,128)(2,1)} %get-tuple-element.23), channel_id=1, source_target_pairs={{0,6},{1,7},{2,4},{3,5},{4,2},{5,3},{6,0},{7,1},{8,14},{9,15},{10,... | collective-permute-start | bytes 196616 | tf_op jit(solution)/shard_map/ppermute | solution.py:203
  58.5 1.6 %collective-permute-start.12 = (bf16[128,256]{1,0:T(8,128)(2,1)}, bf16[128,256]{1,0:T(8,128)(2,1)S(1)}, u32[]{:S(2)}, u32[]{:S(2)}) collective-permute-start(bf16[128,256]{1,0:T(8,128)(2,1)} %get-tuple-element.17.refs_0_.refs_8_), channel_id=1, source_target_pairs={{0,16},{8,24},{16,0},{24,8},{1,17},{9,25},{17,1},{25,9},{2,18},{10... | collective-permute-start | bytes 196616 | tf_op jit(solution)/shard_map/ppermute | solution.py:203
  60.1 1.9 %collective-permute-start.11 = (bf16[128,256]{1,0:T(8,128)(2,1)S(1)}, bf16[128,256]{1,0:T(8,128)(2,1)S(1)}, u32[]{:S(2)}, u32[]{:S(2)}) collective-permute-start(bf16[128,256]{1,0:T(8,128)(2,1)S(1)} %collective-permute-done.10), channel_id=1, source_target_pairs={{0,6},{1,7},{2,4},{3,5},{4,2},{5,3},{6,0},{7,1},{8,14},{9,15},{10,... | collective-permute-start | bytes 196616 | tf_op jit(solution)/shard_map/ppermute | solution.py:203
  62.9 1.6 %collective-permute-start.8 = (bf16[128,256]{1,0:T(8,128)(2,1)S(1)}, bf16[128,256]{1,0:T(8,128)(2,1)S(1)}, u32[]{:S(2)}, u32[]{:S(2)}) collective-permute-start(bf16[128,256]{1,0:T(8,128)(2,1)S(1)} %collective-permute-done.7), channel_id=1, source_target_pairs={{0,4},{1,5},{2,6},{3,7},{4,0},{5,1},{6,2},{7,3},{8,12},{9,13},{10,... | collective-permute-start | bytes 196616 | tf_op jit(solution)/shard_map/ppermute | solution.py:203
  65.0 1.8 %collective-permute-done.11.refs_7_.refs_15_ = bf16[128,256]{1,0:T(8,128)(2,1)S(1)} collective-permute-done((bf16[128,256]{1,0:T(8,128)(2,1)S(1)}, bf16[128,256]{1,0:T(8,128)(2,1)S(1)}, u32[]{:S(2)}, u32[]{:S(2)}) %collective-permute-start.11) | collective-permute-done | bytes 65568 | tf_op jit(solution)/shard_map/ppermute | solution.py:203
  66.8 1.6 %collective-permute-done.5.refs_3_.refs_11_ = bf16[128,256]{1,0:T(8,128)(2,1)S(1)} collective-permute-done((bf16[128,256]{1,0:T(8,128)(2,1)S(1)}, bf16[128,256]{1,0:T(8,128)(2,1)S(1)}, u32[]{:S(2)}, u32[]{:S(2)}) %collective-permute-start.5) | collective-permute-done | bytes 65568 | tf_op jit(solution)/shard_map/ppermute | solution.py:203
  70.1 1.0 collective-permute-start.16
  74.1 1.4 %collective-permute-done.16.refs_10_ = bf16[128,256]{1,0:T(8,128)(2,1)S(1)} collective-permute-done((bf16[128,256]{1,0:T(8,128)(2,1)S(1)}, bf16[128,256]{1,0:T(8,128)(2,1)S(1)}, u32[]{:S(2)}, u32[]{:S(2)}) %collective-permute-start.16) | collective-permute-done | bytes 65568 | tf_op jit(solution)/shard_map/ppermute | solution.py:203
  77.2 1.1 collective-permute-start.18
  79.2 1.1 collective-permute-start.26
  80.8 8.0 %shard_map.40.refs_16_ = f32[2,16,256,1024]{3,2,1,0:T(8,128)} custom-call(s32[1]{0:T(128)} %bitcast.5.place, bf16[128,256]{1,0:T(8,128)(2,1)} %get-tuple-element.17.refs_0_.refs_8_, bf16[128,256]{1,0:T(8,128)(2,1)} %copy-done, bf16[128,256]{1,0:T(8,128)(2,1)} %copy-done.1, bf16[128,256]{1,0:T(8,128)(2,1)} %copy-done.5, bf16[128,256]{1,0:T(8,128)(2,1)} %copy-done.2, ...), custom_call_target="tpu_custom_call" | custom-call | flops 536870912 | bytes 8388608 | tf_op jit(solution)/shard_map/pallas_call | solution.py:183
  90.1 7.6 %shard_map.41.refs_16_ = f32[2,16,256,1024]{3,2,1,0:T(8,128)} custom-call(s32[1]{0:T(128)} %bitcast.4.place, bf16[128,256]{1,0:T(8,128)(2,1)} %get-tuple-element.17.refs_0_.refs_8_, bf16[128,256]{1,0:T(8,128)(2,1)} %copy-done, bf16[128,256]{1,0:T(8,128)(2,1)} %copy-done.1, bf16[128,256]{1,0:T(8,128)(2,1)} %copy-done.5, ...), custom_call_target="tpu_custom_call", output_to_operand_aliasing={{}: (17, {})} | custom-call | flops 536870912 | bytes 8388608 | tf_op jit(solution)/shard_map/pallas_call | solution.py:183
  97.8 7.6 %shard_map.42.refs_16_ = f32[2,16,256,1024]{3,2,1,0:T(8,128)} custom-call(s32[1]{0:T(128)} %bitcast.3.place, bf16[128,256]{1,0:T(8,128)(2,1)} %get-tuple-element.17.refs_0_.refs_8_, bf16[128,256]{1,0:T(8,128)(2,1)} %copy-done, bf16[128,256]{1,0:T(8,128)(2,1)} %copy-done.1, bf16[128,256]{1,0:T(8,128)(2,1)} %copy-done.5, ...), custom_call_target="tpu_custom_call", output_to_operand_aliasing={{}: (17, {})} | custom-call | flops 536870912 | bytes 8388608 | tf_op jit(solution)/shard_map/pallas_call | solution.py:183
  106.2 7.6 %shard_map.43 = f32[2,16,256,1024]{3,2,1,0:T(8,128)} custom-call(s32[1]{0:T(128)} %bitcast.place, bf16[128,256]{1,0:T(8,128)(2,1)} %get-tuple-element.17.refs_0_.refs_8_, bf16[128,256]{1,0:T(8,128)(2,1)} %copy-done, bf16[128,256]{1,0:T(8,128)(2,1)} %copy-done.1, bf16[128,256]{1,0:T(8,128)(2,1)} %copy-done.5, ...), custom_call_target="tpu_custom_call", output_to_operand_aliasing={{}: (17, {})} | custom-call | flops 536870912 | bytes 8388608 | tf_op jit(solution)/shard_map/pallas_call | solution.py:183
  (133 shorter events, 18.3 us)
Async XLA Ops:
  18.9 28.0 %collective-permute-start.1 = (bf16[2,256,256]{2,1,0:T(8,128)(2,1)}, bf16[2,256,256]{2,1,0:T(8,128)(2,1)S(1)}, u32[]{:S(2)}, u32[]{:S(2)}) collective-permute-start(bf16[2,256,256]{2,1,0:T(8,128)(2,1)} %get-tuple-element.16), channel_id=1, source_target_pairs={{0,7},{1,0},{2,1},{3,2},{4,3},{5,4},{6,5},{7,6},{8,15},{9,8},{10,9... | collective-permute-start | bytes 786440 | tf_op jit(solution)/shard_map/ppermute | solution.py:224
  24.9 22.0 %collective-permute-start = (bf16[1,256,256]{2,1,0:T(8,128)(2,1)}, bf16[1,256,256]{2,1,0:T(8,128)(2,1)S(1)}, u32[]{:S(2)}, u32[]{:S(2)}) collective-permute-start(bf16[1,256,256]{2,1,0:T(8,128)(2,1)} %get-tuple-element.15), channel_id=1, source_target_pairs={{0,1},{1,2},{2,3},{3,4},{4,5},{5,6},{6,7},{8,9},{9,10},{10,11},{11... | collective-permute-start | bytes 393224 | tf_op jit(solution)/shard_map/ppermute | solution.py:223
  50.6 6.0 %collective-permute-start.4 = (bf16[128,256]{1,0:T(8,128)(2,1)}, bf16[128,256]{1,0:T(8,128)(2,1)S(1)}, u32[]{:S(2)}, u32[]{:S(2)}) collective-permute-start(bf16[128,256]{1,0:T(8,128)(2,1)} %get-tuple-element.20), channel_id=1, source_target_pairs={{0,1},{1,0},{2,3},{3,2},{4,5},{5,4},{6,7},{7,6},{8,9},{9,8},{10,11... | collective-permute-start | bytes 196616 | tf_op jit(solution)/shard_map/ppermute | solution.py:203
  52.1 6.4 %collective-permute-start.7 = (bf16[128,256]{1,0:T(8,128)(2,1)}, bf16[128,256]{1,0:T(8,128)(2,1)S(1)}, u32[]{:S(2)}, u32[]{:S(2)}) collective-permute-start(bf16[128,256]{1,0:T(8,128)(2,1)} %get-tuple-element.22), channel_id=1, source_target_pairs={{0,1},{1,0},{2,3},{3,2},{4,5},{5,4},{6,7},{7,6},{8,9},{9,8},{10,11... | collective-permute-start | bytes 196616 | tf_op jit(solution)/shard_map/ppermute | solution.py:203
  52.6 5.9 %collective-permute-start.2 = (bf16[128,256]{1,0:T(8,128)(2,1)}, bf16[128,256]{1,0:T(8,128)(2,1)S(1)}, u32[]{:S(2)}, u32[]{:S(2)}) collective-permute-start(bf16[128,256]{1,0:T(8,128)(2,1)} %get-tuple-element.18), channel_id=1, source_target_pairs={{0,1},{1,0},{2,3},{3,2},{4,5},{5,4},{6,7},{7,6},{8,9},{9,8},{10,11... | collective-permute-start | bytes 196616 | tf_op jit(solution)/shard_map/ppermute | solution.py:203
  54.1 6.0 %collective-permute-start.3 = (bf16[128,256]{1,0:T(8,128)(2,1)}, bf16[128,256]{1,0:T(8,128)(2,1)S(1)}, u32[]{:S(2)}, u32[]{:S(2)}) collective-permute-start(bf16[128,256]{1,0:T(8,128)(2,1)} %get-tuple-element.19), channel_id=1, source_target_pairs={{0,2},{1,3},{2,0},{3,1},{4,6},{5,7},{6,4},{7,5},{8,10},{9,11},{10,... | collective-permute-start | bytes 196616 | tf_op jit(solution)/shard_map/ppermute | solution.py:203
  55.2 6.8 %collective-permute-start.6 = (bf16[128,256]{1,0:T(8,128)(2,1)}, bf16[128,256]{1,0:T(8,128)(2,1)S(1)}, u32[]{:S(2)}, u32[]{:S(2)}) collective-permute-start(bf16[128,256]{1,0:T(8,128)(2,1)} %get-tuple-element.21), channel_id=1, source_target_pairs={{0,4},{1,5},{2,6},{3,7},{4,0},{5,1},{6,2},{7,3},{8,12},{9,13},{10,... | collective-permute-start | bytes 196616 | tf_op jit(solution)/shard_map/ppermute | solution.py:203
  56.6 6.3 %collective-permute-start.9 = (bf16[128,256]{1,0:T(8,128)(2,1)}, bf16[128,256]{1,0:T(8,128)(2,1)S(1)}, u32[]{:S(2)}, u32[]{:S(2)}) collective-permute-start(bf16[128,256]{1,0:T(8,128)(2,1)} %get-tuple-element.23), channel_id=1, source_target_pairs={{0,6},{1,7},{2,4},{3,5},{4,2},{5,3},{6,0},{7,1},{8,14},{9,15},{10,... | collective-permute-start | bytes 196616 | tf_op jit(solution)/shard_map/ppermute | solution.py:203
  58.5 6.0 %collective-permute-start.28 = (bf16[128,256]{1,0:T(8,128)(2,1)}, bf16[128,256]{1,0:T(8,128)(2,1)S(1)}, u32[]{:S(2)}, u32[]{:S(2)}) collective-permute-start(bf16[128,256]{1,0:T(8,128)(2,1)} %get-tuple-element.17.refs_0_.refs_8_), channel_id=1, source_target_pairs={{0,8},{8,0},{16,24},{24,16},{1,9},{9,1},{17,25},{25,17},{2,10},{10... | collective-permute-start | bytes 196616 | tf_op jit(solution)/shard_map/ppermute | solution.py:203
  58.5 6.0 %collective-permute-start.12 = (bf16[128,256]{1,0:T(8,128)(2,1)}, bf16[128,256]{1,0:T(8,128)(2,1)S(1)}, u32[]{:S(2)}, u32[]{:S(2)}) collective-permute-start(bf16[128,256]{1,0:T(8,128)(2,1)} %get-tuple-element.17.refs_0_.refs_8_), channel_id=1, source_target_pairs={{0,16},{8,24},{16,0},{24,8},{1,17},{9,25},{17,1},{25,9},{2,18},{10... | collective-permute-start | bytes 196616 | tf_op jit(solution)/shard_map/ppermute | solution.py:203
  60.1 6.7 %collective-permute-start.11 = (bf16[128,256]{1,0:T(8,128)(2,1)S(1)}, bf16[128,256]{1,0:T(8,128)(2,1)S(1)}, u32[]{:S(2)}, u32[]{:S(2)}) collective-permute-start(bf16[128,256]{1,0:T(8,128)(2,1)S(1)} %collective-permute-done.10), channel_id=1, source_target_pairs={{0,6},{1,7},{2,4},{3,5},{4,2},{5,3},{6,0},{7,1},{8,14},{9,15},{10,... | collective-permute-start | bytes 196616 | tf_op jit(solution)/shard_map/ppermute | solution.py:203
  62.0 6.4 %collective-permute-start.5 = (bf16[128,256]{1,0:T(8,128)(2,1)S(1)}, bf16[128,256]{1,0:T(8,128)(2,1)S(1)}, u32[]{:S(2)}, u32[]{:S(2)}) collective-permute-start(bf16[128,256]{1,0:T(8,128)(2,1)S(1)} %collective-permute-done.4), channel_id=1, source_target_pairs={{0,2},{1,3},{2,0},{3,1},{4,6},{5,7},{6,4},{7,5},{8,10},{9,11},{10,... | collective-permute-start | bytes 196616 | tf_op jit(solution)/shard_map/ppermute | solution.py:203
  62.9 6.2 %collective-permute-start.8 = (bf16[128,256]{1,0:T(8,128)(2,1)S(1)}, bf16[128,256]{1,0:T(8,128)(2,1)S(1)}, u32[]{:S(2)}, u32[]{:S(2)}) collective-permute-start(bf16[128,256]{1,0:T(8,128)(2,1)S(1)} %collective-permute-done.7), channel_id=1, source_target_pairs={{0,4},{1,5},{2,6},{3,7},{4,0},{5,1},{6,2},{7,3},{8,12},{9,13},{10,... | collective-permute-start | bytes 196616 | tf_op jit(solution)/shard_map/ppermute | solution.py:203
  64.5 6.6 %collective-permute-start.30 = (bf16[128,256]{1,0:T(8,128)(2,1)S(1)}, bf16[128,256]{1,0:T(8,128)(2,1)S(1)}, u32[]{:S(2)}, u32[]{:S(2)}) collective-permute-start(bf16[128,256]{1,0:T(8,128)(2,1)S(1)} %collective-permute-done.3.refs_2_.refs_10_), channel_id=1, source_target_pairs={{0,8},{8,0},{16,24},{24,16},{1,9},{9,1},{17,25},{25,17},{2,10},{10... | collective-permute-start | bytes 196616 | tf_op jit(solution)/shard_map/ppermute | solution.py:203
  77.2 11.6 %collective-permute-start.18 = (bf16[128,256]{1,0:T(8,128)(2,1)S(1)}, bf16[128,256]{1,0:T(8,128)(2,1)S(1)}, u32[]{:S(2)}, u32[]{:S(2)}) collective-permute-start(bf16[128,256]{1,0:T(8,128)(2,1)S(1)} %collective-permute-done.5.refs_3_.refs_11_), channel_id=1, source_target_pairs={{0,16},{8,24},{16,0},{24,8},{1,17},{9,25},{17,1},{25,9},{2,18},{10... | collective-permute-start | bytes 196616 | tf_op jit(solution)/shard_map/ppermute | solution.py:203
  78.2 10.7 %collective-permute-start.22 = (bf16[128,256]{1,0:T(8,128)(2,1)S(1)}, bf16[128,256]{1,0:T(8,128)(2,1)S(1)}, u32[]{:S(2)}, u32[]{:S(2)}) collective-permute-start(bf16[128,256]{1,0:T(8,128)(2,1)S(1)} %collective-permute-done.8.refs_5_.refs_13_), channel_id=1, source_target_pairs={{0,16},{8,24},{16,0},{24,8},{1,17},{9,25},{17,1},{25,9},{2,18},{10... | collective-permute-start | bytes 196616 | tf_op jit(solution)/shard_map/ppermute | solution.py:203
  79.2 10.2 %collective-permute-start.26 = (bf16[128,256]{1,0:T(8,128)(2,1)S(1)}, bf16[128,256]{1,0:T(8,128)(2,1)S(1)}, u32[]{:S(2)}, u32[]{:S(2)}) collective-permute-start(bf16[128,256]{1,0:T(8,128)(2,1)S(1)} %collective-permute-done.11.refs_7_.refs_15_), channel_id=1, source_target_pairs={{0,16},{8,24},{16,0},{24,8},{1,17},{9,25},{17,1},{25,9},{2,18},{10... | collective-permute-start | bytes 196616 | tf_op jit(solution)/shard_map/ppermute | solution.py:203
  80.3 9.2 %collective-permute-start.15 = (bf16[128,256]{1,0:T(8,128)(2,1)S(1)}, bf16[128,256]{1,0:T(8,128)(2,1)S(1)}, u32[]{:S(2)}, u32[]{:S(2)}) collective-permute-start(bf16[128,256]{1,0:T(8,128)(2,1)S(1)} %collective-permute-done.14.refs_9_), channel_id=1, source_target_pairs={{0,8},{8,0},{16,24},{24,16},{1,9},{9,1},{17,25},{25,17},{2,10},{10... | collective-permute-start | bytes 196616 | tf_op jit(solution)/shard_map/ppermute | solution.py:203
  80.3 9.6 %collective-permute-start.17 = (bf16[128,256]{1,0:T(8,128)(2,1)S(1)}, bf16[128,256]{1,0:T(8,128)(2,1)S(1)}, u32[]{:S(2)}, u32[]{:S(2)}) collective-permute-start(bf16[128,256]{1,0:T(8,128)(2,1)S(1)} %collective-permute-done.16.refs_10_), channel_id=1, source_target_pairs={{0,8},{8,0},{16,24},{24,16},{1,9},{9,1},{17,25},{25,17},{2,10},{10... | collective-permute-start | bytes 196616 | tf_op jit(solution)/shard_map/ppermute | solution.py:203
  88.8 16.6 %collective-permute-start.21 = (bf16[128,256]{1,0:T(8,128)(2,1)S(1)}, bf16[128,256]{1,0:T(8,128)(2,1)S(1)}, u32[]{:S(2)}, u32[]{:S(2)}) collective-permute-start(bf16[128,256]{1,0:T(8,128)(2,1)S(1)} %collective-permute-done.20.refs_12_), channel_id=1, source_target_pairs={{0,8},{8,0},{16,24},{24,16},{1,9},{9,1},{17,25},{25,17},{2,10},{10... | collective-permute-start | bytes 196616 | tf_op jit(solution)/shard_map/ppermute | solution.py:203
  89.0 16.5 %collective-permute-start.25 = (bf16[128,256]{1,0:T(8,128)(2,1)S(1)}, bf16[128,256]{1,0:T(8,128)(2,1)S(1)}, u32[]{:S(2)}, u32[]{:S(2)}) collective-permute-start(bf16[128,256]{1,0:T(8,128)(2,1)S(1)} %collective-permute-done.24.refs_14_), channel_id=1, source_target_pairs={{0,8},{8,0},{16,24},{24,16},{1,9},{9,1},{17,25},{25,17},{2,10},{10... | collective-permute-start | bytes 196616 | tf_op jit(solution)/shard_map/ppermute | solution.py:203
  89.4 16.1 %collective-permute-start.19 = (bf16[128,256]{1,0:T(8,128)(2,1)S(1)}, bf16[128,256]{1,0:T(8,128)(2,1)S(1)}, u32[]{:S(2)}, u32[]{:S(2)}) collective-permute-start(bf16[128,256]{1,0:T(8,128)(2,1)S(1)} %collective-permute-done.18.refs_11_), channel_id=1, source_target_pairs={{0,8},{8,0},{16,24},{24,16},{1,9},{9,1},{17,25},{25,17},{2,10},{10... | collective-permute-start | bytes 196616 | tf_op jit(solution)/shard_map/ppermute | solution.py:203
  89.5 16.0 %collective-permute-start.23 = (bf16[128,256]{1,0:T(8,128)(2,1)S(1)}, bf16[128,256]{1,0:T(8,128)(2,1)S(1)}, u32[]{:S(2)}, u32[]{:S(2)}) collective-permute-start(bf16[128,256]{1,0:T(8,128)(2,1)S(1)} %collective-permute-done.22.refs_13_), channel_id=1, source_target_pairs={{0,8},{8,0},{16,24},{24,16},{1,9},{9,1},{17,25},{25,17},{2,10},{10... | collective-permute-start | bytes 196616 | tf_op jit(solution)/shard_map/ppermute | solution.py:203
  89.9 15.6 %collective-permute-start.27 = (bf16[128,256]{1,0:T(8,128)(2,1)S(1)}, bf16[128,256]{1,0:T(8,128)(2,1)S(1)}, u32[]{:S(2)}, u32[]{:S(2)}) collective-permute-start(bf16[128,256]{1,0:T(8,128)(2,1)S(1)} %collective-permute-done.26.refs_15_), channel_id=1, source_target_pairs={{0,8},{8,0},{16,24},{24,16},{1,9},{9,1},{17,25},{25,17},{2,10},{10... | collective-permute-start | bytes 196616 | tf_op jit(solution)/shard_map/ppermute | solution.py:203
  (45 other events, 494.8 us)

commit v2 on v0

v2 whole, which is shorter than its diff:
```python
import functools

import jax
import jax.numpy as jnp
import numpy as np
from jax import lax
from jax.experimental import pallas as pl
from jax.experimental.pallas import tpu as pltpu
from jax.sharding import PartitionSpec as P

TRANSFORM = 8192
TAPS = 4
LANES = 128
SUB = 128
DEPTH = 512
PER_STEP = 2
CHUNK = 16
VMEM = 60 * 1024 * 1024
PIECES = 2


def prototype():
    sample = np.arange(TAPS * TRANSFORM, dtype=np.float64).reshape(TAPS, TRANSFORM)[:, : TRANSFORM // 2]
    offset = (sample + 0.5) / TRANSFORM - TAPS / 2.0
    window = 0.5 - 0.5 * np.cos(2.0 * np.pi * (sample + 0.5) / (TAPS * TRANSFORM))
    return (np.sinc(offset) * window).astype(np.float32)


def angle_tables(kept_channels):
    circle = 2 * TRANSFORM
    row = jnp.arange(SUB + TRANSFORM // 2 // SUB, dtype=jnp.int32)
    twice = jnp.where(row < SUB, 2 * row + 1, 2 * SUB * (row - SUB))[:, None]
    angles = (kept_channels[None, :] * twice % circle).astype(jnp.float32) * (2.0 * jnp.pi / circle)
    return jnp.cos(angles), jnp.sin(angles)


def dft_kernel(planes, frames, groups, *refs):
    nf, ng = len(frames), len(groups)
    ahead, mirror = refs[:nf], refs[nf : 2 * nf]
    coeff, cos_c, sin_c, cos_f, sin_f, codes = refs[2 * nf : 2 * nf + 6]
    outs, refs = refs[2 * nf + 6 : 2 * nf + 6 + ng], refs[2 * nf + 6 + ng :]
    acc_even, acc_odd = refs[:2]
    rows = ahead[0].shape[0]
    kept = cos_f.shape[1]
    step = pl.program_id(0)
    low = [p for p, (_, wanted) in enumerate(planes) if wanted]
    place = {p: (len(planes) + i) * rows for i, p in enumerate(low)}
    width = 2 * LANES
    span = DEPTH * PER_STEP
    backwards = LANES - 1 - lax.broadcasted_iota(jnp.int32, (CHUNK, LANES), 1)

    @pl.when(step == 0)
    def _():
        acc_even[...] = jnp.zeros_like(acc_even)
        acc_odd[...] = jnp.zeros_like(acc_odd)

    for u in range(PER_STEP):
        even, odd, t_even, t_odd = refs[2 + 4 * u : 6 + 4 * u]
        for b in range(DEPTH // SUB):
            block = u * (DEPTH // SUB) + b
            for q in range(0, SUB, CHUNK):
                here = slice(b * SUB + q, b * SUB + q + CHUNK)
                cos_b, sin_b = cos_c[block : block + 1, :], sin_c[block : block + 1, :]
                cos_q, sin_q = cos_f[q : q + CHUNK, :], sin_f[q : q + CHUNK, :]
                for held, table in (
                    (t_even, cos_b * cos_q - sin_b * sin_q),
                    (t_odd, sin_b * cos_q + cos_b * sin_q),
                ):
                    high = table.astype(jnp.bfloat16)
                    held[here, :kept] = high
                    held[here, kept:] = (table - high.astype(jnp.float32)).astype(jnp.bfloat16)
        for w in range(0, DEPTH, width):
            at = u * DEPTH + w
            taps = [jnp.broadcast_to(coeff[t : t + 1, at : at + width], (CHUNK, width)) for t in range(TAPS)]
            for r in range(0, rows, CHUNK):
                fore, rear = {}, {}
                for i, f in enumerate(frames):
                    fore[f] = ahead[i][r : r + CHUNK, at : at + width].astype(jnp.float32)
                    seen = mirror[i][r : r + CHUNK, span - at - width : span - at].astype(jnp.float32)
                    rear[f] = jnp.concatenate(
                        [
                            jnp.take_along_axis(seen[:, c : c + LANES], backwards, axis=1)
                            for c in range(width - LANES, -1, -LANES)
                        ],
                        axis=1,
                    )
                for p, (s, _) in enumerate(planes):
                    x = z = None
                    for t in range(TAPS):
                        f = s - (TAPS - 1) + t
                        if f in fore:
                            a, b = taps[t] * fore[f], taps[TAPS - 1 - t] * rear[f]
                            x, z = (a, b) if x is None else (x + a, z + b)
                    for value, held in ((x + z, even), (x - z, odd)):
                        high = value.astype(jnp.bfloat16)
                        held[p * rows + r : p * rows + r + CHUNK, w : w + width] = high
                        if p in place:
                            rest = (value - high.astype(jnp.float32)).astype(jnp.bfloat16)
                            held[place[p] + r : place[p] + r + CHUNK, w : w + width] = rest
        acc_even[...] += jnp.dot(even[...], t_even[...], preferred_element_type=jnp.float32)
        acc_odd[...] += jnp.dot(odd[...], t_odd[...], preferred_element_type=jnp.float32)

    @pl.when(step == pl.num_programs(0) - 1)
    def _():
        def total(acc, p):
            value = acc[p * rows : (p + 1) * rows, :kept] + acc[p * rows : (p + 1) * rows, kept:]
            if p in place:
                rest = slice(place[p], place[p] + rows)
                value = value + acc[rest, :kept] + acc[rest, kept:]
            return value

        cos_h, sin_h = cos_f[0:1, :], sin_f[0:1, :]
        scale = codes[...].astype(jnp.float32) * (TRANSFORM**-0.5 / 16.0)
        for out, (members, dtype) in zip(outs, groups):
            for i, p in enumerate(members):
                even, odd = total(acc_even, p), total(acc_odd, p)
                out[i, :kept] = ((cos_h * even + sin_h * odd).T * scale).astype(dtype)
                out[i, kept:] = ((sin_h * even - cos_h * odd).T * scale).astype(dtype)


def spectra(voltages, coeffs, tables, codes, planes, groups, piece=0, pieces=1):
    rows = voltages.shape[0] // pieces
    own = voltages.shape[1] // TRANSFORM
    span = DEPTH * PER_STEP
    steps = TRANSFORM // 2 // span
    kept = tables[0].shape[1]
    columns = 2 * kept
    frames = sorted({s - (TAPS - 1) + t for s, _ in planes for t in range(TAPS)} & set(range(own)))
    count = len(planes) + sum(wanted for _, wanted in planes)

    def ahead(f):
        return pl.BlockSpec((rows, span), lambda j: (piece, 2 * f * steps + j))

    def mirror(f):
        return pl.BlockSpec((rows, span), lambda j: (piece, 2 * f * steps + 2 * steps - 1 - j))

    coarse = pl.BlockSpec((span // SUB, kept), lambda j: (SUB // (span // SUB) + j, 0))
    fine = pl.BlockSpec((SUB, kept), lambda j: (0, 0))
    cos_t, sin_t = tables
    outs = [jax.ShapeDtypeStruct((len(m), columns, rows), d) for m, d in groups]
    part = [
        pltpu.VMEM((count * rows, DEPTH), jnp.bfloat16),
        pltpu.VMEM((count * rows, DEPTH), jnp.bfloat16),
        pltpu.VMEM((DEPTH, columns), jnp.bfloat16),
        pltpu.VMEM((DEPTH, columns), jnp.bfloat16),
    ]
    return pl.pallas_call(
        functools.partial(dft_kernel, planes, frames, groups),
        grid=(steps,),
        in_specs=[ahead(f) for f in frames]
        + [mirror(f) for f in frames]
        + [pl.BlockSpec((TAPS, span), lambda j: (0, j)), coarse, coarse, fine, fine]
        + [pl.BlockSpec((1, rows), lambda j: (0, piece))],
        out_specs=[pl.BlockSpec(o.shape, lambda j: (0, 0, 0)) for o in outs],
        out_shape=outs,
        scratch_shapes=[pltpu.VMEM((count * rows, columns), jnp.float32)] * 2 + part * PER_STEP,
        compiler_params=pltpu.CompilerParams(vmem_limit_bytes=VMEM),
        cost_estimate=pl.CostEstimate(
            flops=2 * rows * TRANSFORM * columns * count,
            bytes_accessed=len(frames) * rows * TRANSFORM * 2,
            transcendentals=0,
        ),
    )(*[voltages] * (2 * len(frames)), coeffs, cos_t, sin_t, cos_t, sin_t, codes)


def combine_kernel(parts, place, own, ahead, behind, out, mixed):
    me = place[0]
    slots, columns = own.shape[0], own.shape[1]
    kept = columns // 2
    inside = jnp.where(me == parts - 1, 0.0, 1.0)
    back = behind.shape[0]
    for s in range(slots):
        value = own[s]
        if s == 0:
            value = value + ahead[0].astype(jnp.float32)
        if s >= slots - back:
            value = value * inside + behind[s - (slots - back)].astype(jnp.float32)
        for p in range(2):
            for h in range(mixed.shape[0]):
                mixed[h, pl.ds(p * slots + s, kept, stride=2 * slots), :] = value[
                    p * kept : (p + 1) * kept, h * LANES : (h + 1) * LANES
                ]
    for h in range(mixed.shape[0]):
        for i in range(out.shape[0]):
            rows = out.shape[1]
            out[i, :, h * LANES : (h + 1) * LANES] = mixed[h, i * rows : (i + 1) * rows, :].astype(out.dtype)


def combined(parts, me, own, ahead, behind, piece):
    slots, columns, rows = own.shape
    block = columns * slots // parts

    def arriving(x):
        return pl.BlockSpec((x.shape[0], columns, rows), lambda j: (0, 0, piece))

    return pl.pallas_call(
        functools.partial(combine_kernel, parts),
        grid=(1,),
        in_specs=[pl.BlockSpec(memory_space=pltpu.SMEM), pl.BlockSpec(own.shape, lambda j: (0, 0, 0))]
        + [arriving(ahead), arriving(behind)],
        out_specs=pl.BlockSpec((parts, block, rows), lambda j: (0, 0, 0)),
        out_shape=jax.ShapeDtypeStruct((parts, block, rows), jnp.bfloat16),
        scratch_shapes=[pltpu.VMEM((rows // LANES, slots * columns, LANES), jnp.float32)],
        compiler_params=pltpu.CompilerParams(vmem_limit_bytes=VMEM),
    )(me, own, ahead, behind)


def correlate_kernel(half, pair, spectra_count, pieces, sets, groups, seat, *refs):
    out = refs[-1]
    wide = 2 * half
    step = pl.program_id(0)
    tile = 16 // wide
    me = seat[0]

    def gathered(tiles, take):
        return jnp.concatenate([jnp.concatenate([t[take] for t in p], axis=0) for p in tiles], axis=1)

    for group in range(pair // tile):
        at = pl.multiple_of((step * pair + group * tile) * wide, 16)
        tiles = [
            [
                [
                    refs[(m * pieces + p) * sets + k][i, pl.ds(at, 16), :].astype(jnp.float32)
                    for k in range(sets)
                    for i in range(refs[k].shape[0])
                ]
                for p in range(pieces)
            ]
            for m in range(groups)
        ]
        for h in range(tile):
            c = group * tile + h
            columns = [gathered(t, slice(h * wide, (h + 1) * wide)) for t in tiles]
            left = columns[0]
            bit = 1
            while bit < groups:
                swap = (me // bit) % 2 == 1
                columns = [jnp.where(swap, columns[q ^ bit], columns[q]) for q in range(groups)]
                bit *= 2
            right = jnp.concatenate(columns, axis=1).astype(jnp.bfloat16)
            row = lax.broadcasted_iota(jnp.int32, left.shape, 0) % wide
            turned = jnp.where(row < half, pltpu.roll(left, left.shape[0] - half, 0), -pltpu.roll(left, half, 0))
            both = jnp.concatenate([left.T, turned.T], axis=0).astype(jnp.bfloat16)
            result = jnp.dot(both, right, preferred_element_type=jnp.float32) * (1.0 / spectra_count)
            out[0, c], out[1, c] = result[: left.shape[1]], result[left.shape[1] :]


def correlated(seat, seen, half, spectra_count):
    groups, pieces, sets = len(seen), len(seen[0]), len(seen[0][0])
    wide = 2 * half
    block = seen[0][0][0].shape[1]
    rows = sum(p[0].shape[2] for p in seen[0])
    channels = block // wide
    pair = min(channels, 16 // wide)
    arrays = [a for mask in seen for piece in mask for a in piece]
    return pl.pallas_call(
        functools.partial(correlate_kernel, half, pair, spectra_count, pieces, sets, groups),
        grid_spec=pltpu.PrefetchScalarGridSpec(
            num_scalar_prefetch=1,
            grid=(channels // pair,),
            in_specs=[pl.BlockSpec(a.shape, lambda j, seat: (0, 0, 0)) for a in arrays],
            out_specs=pl.BlockSpec((2, pair, rows, groups * rows), lambda j, seat: (0, j, 0, 0)),
        ),
        out_shape=jax.ShapeDtypeStruct((2, channels, rows, groups * rows), jnp.float32),
        compiler_params=pltpu.CompilerParams(vmem_limit_bytes=VMEM),
        cost_estimate=pl.CostEstimate(
            flops=8 * spectra_count * rows * groups * rows * channels,
            bytes_accessed=2 * channels * rows * groups * rows * 4,
            transcendentals=0,
        ),
    )(seat, *arrays)


def exchanged(block, axis, mask):
    return lax.ppermute(block, axis, [(i, i ^ mask) for i in range(lax.axis_size(axis))])


def local(voltages, scale_codes, kept_channels):
    rows = voltages.shape[0]
    own = voltages.shape[1] // TRANSFORM
    history = TAPS - 1
    parts, groups = lax.axis_size("chan"), lax.axis_size("inp")
    me, seat = lax.axis_index("chan"), lax.axis_index("inp")
    coeffs = prototype()
    tables = angle_tables(kept_channels)
    codes = scale_codes[None, :]
    first = 2
    last = first + own
    edge = [(s, False) for s in [*range(first), *range(last, own + history)]]
    inner = [(s, s < last - 1) for s in range(first, last)]
    behind, ahead = spectra(
        voltages, coeffs, tables, codes, edge,
        [(list(range(first)), jnp.bfloat16), (list(range(first, len(edge))), jnp.bfloat16)],
    )
    ahead = lax.ppermute(ahead, "chan", [(i, i + 1) for i in range(parts - 1)])
    behind = lax.ppermute(behind, "chan", [(i, (i - 1) % parts) for i in range(parts)])
    me, seat = me.astype(jnp.int32).reshape(1), seat.astype(jnp.int32).reshape(1)
    mine = []
    for piece in range(PIECES):
        (planes,) = spectra(voltages, coeffs, tables, codes, inner, [(list(range(own)), jnp.float32)], piece, PIECES)
        blocks = combined(parts, me, planes, ahead, behind, piece)
        mine.append([lax.all_to_all(blocks, "chan", 0, 0, tiled=True)])
    seen = {0: mine}
    bit = groups // 2
    while bit:
        seen.update({m | bit: [[exchanged(b, "inp", bit) for b in p] for p in seen[m]] for m in list(seen)})
        bit //= 2
    return correlated(seat, [seen[m] for m in range(groups)], own, own * parts)


def solution(mesh):
    placed = (P("inp", "chan"), P("inp"), P())
    return jax.shard_map(
        local, mesh=mesh, in_specs=placed, out_specs=P(None, "chan", "inp", None), check_vma=False
    )
```

time: 264 us -> 89.3 us (0.34)
  other arithmetic: 113 us -> 1.73 us
  matrix products: 66.1 us -> 0 us
  Pallas kernels: 0 us -> 52.3 us
  waiting for transfers between devices: 38.8 us -> 12.5 us
  blocking collectives: 20.2 us -> 0 us
  starting transfers between devices: 4.92 us -> 20.8 us
  between operations: 13.5 us -> 0.13 us
  local copies, waits for them, and re-layouts: 6.21 us -> 1.4 us
    dot_general x3 -> x0, matrix products: 66.1 us -> none  [the longest x1 58.1 us: transform(): jnp.einsum('isn,nkp->kspi', filtered, transform_table, precision=lax.Prec...]
    mul x2 -> x0, other arithmetic: 55.2 us -> none  [the longest x1 54.6 us: local(): coeffs[tap_index][None, None, :] * frames.astype(jnp.float32)]
    pallas_call x0 -> x6, Pallas kernels: none -> 52.3 us  [the longest x3 34.4 us: spectra(): pl.pallas_call(functools.partial(dft_kernel, planes, frames, groups), gri...]
    all_gather x1 -> x0, waiting for transfers between devices: 22.1 us -> none  [local(): columns = lax.all_gather(turned, 'inp', axis=2, tiled=True)]
    all_to_all x1 -> x0, blocking collectives: 20.2 us -> none  [local(): lax.all_to_all(channelized, 'chan', split_axis=0, concat_axis=1, tiled=True)]
    cos x1 -> x0, other arithmetic: 19 us -> none  [dft_table(): return jnp.stack([jnp.cos(angles), -jnp.sin(angles)], axis=-1) * norming]
    convert_element_type x2 -> x0, other arithmetic: 18.4 us -> none  [the longest x1 18.3 us: local(): frames.astype(jnp.float32)]
    div x2 -> x0, other arithmetic: 11.7 us -> none  [the longest x1 11.7 us: local(): return jnp.stack([real_part, imag_part]) / spectra_count]
  transfers between devices with their start and end apart: 2 -> 10, of which waited for: 2 -> 3; matrix products, arithmetic and copies ran while one was open for 0% -> 0% of each run, Pallas kernels for 0% -> 29%
where the time goes in v2:
time: 89.3 us; the launch traced here: 88.9 us
  Pallas kernels  52.3 us (59%)
  starting transfers between devices  20.8 us (23%)
  waiting for transfers between devices  12.5 us (14%)
  other arithmetic  1.73 us (2%)
  local copies, waits for them, and re-layouts  1.4 us (2%)
    pallas_call x3, Pallas kernels, spectra(): pl.pallas_call(functools.partial(dft_kernel, planes, frames, groups), gri...  34.4 us
    pallas_call x1, Pallas kernels, correlated(): pl.pallas_call(functools.partial(correlate_kernel, half, pair, spectra_co...  14 us
    all_to_all x2, starting transfers between devices, local(): mine.append([lax.all_to_all(blocks, 'chan', 0, 0, tiled=True)])  9.93 us
    all_to_all x2, waiting for transfers between devices, local(): mine.append([lax.all_to_all(blocks, 'chan', 0, 0, tiled=True)])  6.74 us
    ppermute x6, waiting for transfers between devices, exchanged(): lax.ppermute(block, axis, [(i, i ^ mask) for i in range(lax.axis_size(axi...  5.78 us
    ppermute x1, starting transfers between devices, local(): ahead = lax.ppermute(ahead, 'chan', [(i, i + 1) for i in range(parts - 1)])  4.87 us
    pallas_call x2, Pallas kernels, combined(): pl.pallas_call(functools.partial(combine_kernel, parts), grid=(1,), in_sp...  3.92 us
    ppermute x6, starting transfers between devices, exchanged(): lax.ppermute(block, axis, [(i, i ^ mask) for i in range(lax.axis_size(axi...  3.56 us
  transfers between devices with their start and end apart: 10, of which 3 were waited for; matrix products, arithmetic and copies ran while one was open for 0% of the time, Pallas kernels for 29%

profile of v2, /device:TPU:0, one launch (start us, length us, event | category | flops | bytes accessed | tf_op | source)
XLA Modules:
  0.0 88.9 jit_solution(929686350884796971)
XLA Ops:
  0.0 1.7 %fusion.3 = (f32[160,128]{1,0:T(8,128)}, f32[160,128]{1,0:T(8,128)}) fusion(s32[160]{0:T(256)S(1)} %fusion.5, s32[128]{0:T(128)} %param.6), kind=kLoop, calls=%fused_computation.8 | loop fusion | flops 286720 | bytes 164992 | tf_op jit(solution)/shard_map/sin | solution.py:34
  1.7 10.8 %shard_map.47 = (bf16[2,256,256]{2,1,0:T(8,128)(2,1)}, bf16[1,256,256]{2,1,0:T(8,128)(2,1)}) custom-call(bf16[256,32768]{1,0:T(8,128)(2,1)} %refs_7_.3, bf16[256,32768]{1,0:T(8,128)(2,1)} %refs_7_.3, bf16[256,32768]{1,0:T(8,128)(2,1)} %refs_7_.3, bf16[256,32768]{1,0:T(8,128)(2,1)} %refs_7_.3, bf16[256,32768]{1,0:T(8,128)(2,1)} %refs_7_.3, ...), custom_call_target="tpu_custom_call" | custom-call | flops 3221225472 | bytes 12582912 | tf_op jit(solution)/shard_map/pallas_call | solution.py:147
  12.5 4.9 %collective-permute-start = (bf16[1,256,256]{2,1,0:T(8,128)(2,1)}, bf16[1,256,256]{2,1,0:T(8,128)(2,1)S(1)}, u32[]{:S(2)}, u32[]{:S(2)}) collective-permute-start(bf16[1,256,256]{2,1,0:T(8,128)(2,1)} %get-tuple-element.7), channel_id=1, source_target_pairs={{0,1},{1,2},{2,3},{3,4},{4,5},{5,6},{6,7},{8,9},{9,10},{10,11},{11... | collective-permute-start | bytes 393224 | tf_op jit(solution)/shard_map/ppermute | solution.py:295
  17.4 2.5 %collective-permute-start.1 = (bf16[2,256,256]{2,1,0:T(8,128)(2,1)}, bf16[2,256,256]{2,1,0:T(8,128)(2,1)S(1)}, u32[]{:S(2)}, u32[]{:S(2)}) collective-permute-start(bf16[2,256,256]{2,1,0:T(8,128)(2,1)} %get-tuple-element.8), channel_id=1, source_target_pairs={{0,7},{1,0},{2,1},{3,2},{4,3},{5,4},{6,5},{7,6},{8,15},{9,8},{10,9... | collective-permute-start | bytes 786440 | tf_op jit(solution)/shard_map/ppermute | solution.py:296
  19.8 11.8 %shard_map.49.own = f32[4,256,128]{2,1,0:T(8,128)} custom-call(bf16[256,32768]{1,0:T(8,128)(2,1)} %refs_7_.3, bf16[256,32768]{1,0:T(8,128)(2,1)} %refs_7_.3, bf16[256,32768]{1,0:T(8,128)(2,1)} %refs_7_.3, bf16[256,32768]{1,0:T(8,128)(2,1)} %refs_7_.3, bf16[256,32768]{1,0:T(8,128)(2,1)} %refs_7_.3, bf16[256,32768]{1,0:T(8,128)(2,1)} %refs_7_.3, ...), custom_call_target="tpu_custom_call" | custom-call | flops 3758096384 | bytes 8388608 | tf_op jit(solution)/shard_map/pallas_call | solution.py:147
  31.7 0.0 collective-permute-done.ahead
  31.7 0.6 copy-done.3
  32.3 0.1 copy-done.2
  32.4 2.0 %shard_map.50 = bf16[8,128,128]{2,1,0:T(8,128)(2,1)} custom-call(s32[1]{0:T(128)} %bitcast.1.place, f32[4,256,128]{2,1,0:T(8,128)} %shard_map.49.own, bf16[1,256,256]{2,1,0:T(8,128)(2,1)} %copy-done.3, bf16[2,256,256]{2,1,0:T(8,128)(2,1)} %copy-done.2), custom_call_target="tpu_custom_call" | custom-call | tf_op jit(solution)/shard_map/pallas_call | solution.py:196
  34.4 3.9 %all-to-all-start.1 = ((bf16[8,128,128]{2,1,0:T(8,128)(2,1)}), bf16[8,128,128]{2,1,0:T(8,128)(2,1)S(1)}, u32[]{:S(2)}, u32[]{:S(2)}) async-start(bf16[8,128,128]{2,1,0:T(8,128)(2,1)} %shard_map.50), calls=%async_computation.1 | async-start | bytes 524288 | tf_op jit(solution)/shard_map/all_to_all | solution.py:302
  38.3 11.8 %shard_map.46.own = f32[4,256,128]{2,1,0:T(8,128)} custom-call(bf16[256,32768]{1,0:T(8,128)(2,1)} %refs_7_.3, bf16[256,32768]{1,0:T(8,128)(2,1)} %refs_7_.3, bf16[256,32768]{1,0:T(8,128)(2,1)} %refs_7_.3, bf16[256,32768]{1,0:T(8,128)(2,1)} %refs_7_.3, bf16[256,32768]{1,0:T(8,128)(2,1)} %refs_7_.3, bf16[256,32768]{1,0:T(8,128)(2,1)} %refs_7_.3, ...), custom_call_target="tpu_custom_call" | custom-call | flops 3758096384 | bytes 8388608 | tf_op jit(solution)/shard_map/pallas_call | solution.py:147
  50.1 2.0 %shard_map.48 = bf16[8,128,128]{2,1,0:T(8,128)(2,1)} custom-call(s32[1]{0:T(128)} %bitcast.1.place, f32[4,256,128]{2,1,0:T(8,128)} %shard_map.46.own, bf16[1,256,256]{2,1,0:T(8,128)(2,1)} %copy-done.3, bf16[2,256,256]{2,1,0:T(8,128)(2,1)} %copy-done.2), custom_call_target="tpu_custom_call" | custom-call | tf_op jit(solution)/shard_map/pallas_call | solution.py:196
  52.0 0.0 all-to-all-done.1.refs_1_
  52.0 6.0 %all-to-all-start = ((bf16[8,128,128]{2,1,0:T(8,128)(2,1)}), bf16[8,128,128]{2,1,0:T(8,128)(2,1)S(1)}, u32[]{:S(2)}, u32[]{:S(2)}) async-start(bf16[8,128,128]{2,1,0:T(8,128)(2,1)} %shard_map.48), calls=%async_computation | async-start | bytes 524288 | tf_op jit(solution)/shard_map/all_to_all | solution.py:302
  58.1 1.5 %collective-permute-start.5 = (bf16[8,128,128]{2,1,0:T(8,128)(2,1)S(1)}, bf16[8,128,128]{2,1,0:T(8,128)(2,1)S(1)}, u32[]{:S(2)}, u32[]{:S(2)}) collective-permute-start(bf16[8,128,128]{2,1,0:T(8,128)(2,1)S(1)} %all-to-all-done.1.refs_1_), channel_id=1, source_target_pairs={{0,16},{8,24},{16,0},{24,8},{1,17},{9,25},{17,1},{25,9},{2,18},{10... | collective-permute-start | bytes 786440 | tf_op jit(solution)/shard_map/ppermute | solution.py:275
  59.5 6.7 %all-to-all-done.refs_0_ = bf16[8,128,128]{2,1,0:T(8,128)(2,1)S(1)} async-done(((bf16[8,128,128]{2,1,0:T(8,128)(2,1)}), bf16[8,128,128]{2,1,0:T(8,128)(2,1)S(1)}, u32[]{:S(2)}, u32[]{:S(2)}) %all-to-all-start) | async-done | bytes 262176 | tf_op jit(solution)/shard_map/all_to_all | solution.py:302
  66.3 1.5 %collective-permute-start.4 = (bf16[8,128,128]{2,1,0:T(8,128)(2,1)S(1)}, bf16[8,128,128]{2,1,0:T(8,128)(2,1)S(1)}, u32[]{:S(2)}, u32[]{:S(2)}) collective-permute-start(bf16[8,128,128]{2,1,0:T(8,128)(2,1)S(1)} %all-to-all-done.refs_0_), channel_id=1, source_target_pairs={{0,16},{8,24},{16,0},{24,8},{1,17},{9,25},{17,1},{25,9},{2,18},{10... | collective-permute-start | bytes 786440 | tf_op jit(solution)/shard_map/ppermute | solution.py:275
  67.8 0.5 collective-permute-start.2
  68.3 0.0 collective-permute-done.5.refs_5_
  68.3 0.1 collective-permute-start.7
  68.4 4.3 %collective-permute-done.4.refs_4_ = bf16[8,128,128]{2,1,0:T(8,128)(2,1)S(1)} collective-permute-done((bf16[8,128,128]{2,1,0:T(8,128)(2,1)S(1)}, bf16[8,128,128]{2,1,0:T(8,128)(2,1)S(1)}, u32[]{:S(2)}, u32[]{:S(2)}) %collective-permute-start.4) | collective-permute-done | bytes 262176 | tf_op jit(solution)/shard_map/ppermute | solution.py:275
  72.7 1.5 %collective-permute-done.6.refs_6_ = bf16[8,128,128]{2,1,0:T(8,128)(2,1)S(1)} collective-permute-done((bf16[8,128,128]{2,1,0:T(8,128)(2,1)S(1)}, bf16[8,128,128]{2,1,0:T(8,128)(2,1)S(1)}, u32[]{:S(2)}, u32[]{:S(2)}) %collective-permute-start.6) | collective-permute-done | bytes 262176 | tf_op jit(solution)/shard_map/ppermute | solution.py:275
  74.2 0.6 copy-done.9
  74.9 14.0 %shard_map.51 = f32[2,16,256,1024]{3,2,1,0:T(8,128)} custom-call(s32[1]{0:T(128)} %bitcast.seat, bf16[8,128,128]{2,1,0:T(8,128)(2,1)} %copy-done.1, bf16[8,128,128]{2,1,0:T(8,128)(2,1)} %copy-done, bf16[8,128,128]{2,1,0:T(8,128)(2,1)} %copy-done.7, bf16[8,128,128]{2,1,0:T(8,128)(2,1)} %copy-done.6, bf16[8,128,128]{2,1,0:T(8,128)(2,1)} %copy-done.5, ...), custom_call_target="tpu_custom_call" | custom-call | flops 1073741824 | bytes 33554432 | tf_op jit(solution)/shard_map/pallas_call | solution.py:256
  (24 shorter events, 0.1 us)
Async XLA Ops:
  12.5 19.2 %collective-permute-start = (bf16[1,256,256]{2,1,0:T(8,128)(2,1)}, bf16[1,256,256]{2,1,0:T(8,128)(2,1)S(1)}, u32[]{:S(2)}, u32[]{:S(2)}) collective-permute-start(bf16[1,256,256]{2,1,0:T(8,128)(2,1)} %get-tuple-element.7), channel_id=1, source_target_pairs={{0,1},{1,2},{2,3},{3,4},{4,5},{5,6},{6,7},{8,9},{9,10},{10,11},{11... | collective-permute-start | bytes 393224 | tf_op jit(solution)/shard_map/ppermute | solution.py:295
  17.4 14.3 %collective-permute-start.1 = (bf16[2,256,256]{2,1,0:T(8,128)(2,1)}, bf16[2,256,256]{2,1,0:T(8,128)(2,1)S(1)}, u32[]{:S(2)}, u32[]{:S(2)}) collective-permute-start(bf16[2,256,256]{2,1,0:T(8,128)(2,1)} %get-tuple-element.8), channel_id=1, source_target_pairs={{0,7},{1,0},{2,1},{3,2},{4,3},{5,4},{6,5},{7,6},{8,15},{9,8},{10,9... | collective-permute-start | bytes 786440 | tf_op jit(solution)/shard_map/ppermute | solution.py:296
  31.7 0.7 copy-start.3
  31.7 0.7 copy-start.2
  34.4 17.7 %all-to-all-start.1 = ((bf16[8,128,128]{2,1,0:T(8,128)(2,1)}), bf16[8,128,128]{2,1,0:T(8,128)(2,1)S(1)}, u32[]{:S(2)}, u32[]{:S(2)}) async-start(bf16[8,128,128]{2,1,0:T(8,128)(2,1)} %shard_map.50), calls=%async_computation.1 | async-start | bytes 524288 | tf_op jit(solution)/shard_map/all_to_all | solution.py:302
  52.0 22.2 %copy-start = (bf16[8,128,128]{2,1,0:T(8,128)(2,1)}, bf16[8,128,128]{2,1,0:T(8,128)(2,1)S(1)}, u32[]{:S(2)}) copy-start(bf16[8,128,128]{2,1,0:T(8,128)(2,1)S(1)} %all-to-all-done.1.refs_1_) | copy-start | bytes 786436
  52.0 14.2 %all-to-all-start = ((bf16[8,128,128]{2,1,0:T(8,128)(2,1)}), bf16[8,128,128]{2,1,0:T(8,128)(2,1)S(1)}, u32[]{:S(2)}, u32[]{:S(2)}) async-start(bf16[8,128,128]{2,1,0:T(8,128)(2,1)} %shard_map.48), calls=%async_computation | async-start | bytes 524288 | tf_op jit(solution)/shard_map/all_to_all | solution.py:302
  58.1 10.2 %collective-permute-start.5 = (bf16[8,128,128]{2,1,0:T(8,128)(2,1)S(1)}, bf16[8,128,128]{2,1,0:T(8,128)(2,1)S(1)}, u32[]{:S(2)}, u32[]{:S(2)}) collective-permute-start(bf16[8,128,128]{2,1,0:T(8,128)(2,1)S(1)} %all-to-all-done.1.refs_1_), channel_id=1, source_target_pairs={{0,16},{8,24},{16,0},{24,8},{1,17},{9,25},{17,1},{25,9},{2,18},{10... | collective-permute-start | bytes 786440 | tf_op jit(solution)/shard_map/ppermute | solution.py:275
  66.3 7.9 %copy-start.1 = (bf16[8,128,128]{2,1,0:T(8,128)(2,1)}, bf16[8,128,128]{2,1,0:T(8,128)(2,1)S(1)}, u32[]{:S(2)}) copy-start(bf16[8,128,128]{2,1,0:T(8,128)(2,1)S(1)} %all-to-all-done.refs_0_) | copy-start | bytes 786436
  66.3 6.4 %collective-permute-start.4 = (bf16[8,128,128]{2,1,0:T(8,128)(2,1)S(1)}, bf16[8,128,128]{2,1,0:T(8,128)(2,1)S(1)}, u32[]{:S(2)}, u32[]{:S(2)}) collective-permute-start(bf16[8,128,128]{2,1,0:T(8,128)(2,1)S(1)} %all-to-all-done.refs_0_), channel_id=1, source_target_pairs={{0,16},{8,24},{16,0},{24,8},{1,17},{9,25},{17,1},{25,9},{2,18},{10... | collective-permute-start | bytes 786440 | tf_op jit(solution)/shard_map/ppermute | solution.py:275
  67.8 4.9 %collective-permute-start.3 = (bf16[8,128,128]{2,1,0:T(8,128)(2,1)S(1)}, bf16[8,128,128]{2,1,0:T(8,128)(2,1)S(1)}, u32[]{:S(2)}, u32[]{:S(2)}) collective-permute-start(bf16[8,128,128]{2,1,0:T(8,128)(2,1)S(1)} %all-to-all-done.1.refs_1_), channel_id=1, source_target_pairs={{0,8},{8,0},{16,24},{24,16},{1,9},{9,1},{17,25},{25,17},{2,10},{10... | collective-permute-start | bytes 786440 | tf_op jit(solution)/shard_map/ppermute | solution.py:275
  67.8 4.9 %collective-permute-start.2 = (bf16[8,128,128]{2,1,0:T(8,128)(2,1)S(1)}, bf16[8,128,128]{2,1,0:T(8,128)(2,1)S(1)}, u32[]{:S(2)}, u32[]{:S(2)}) collective-permute-start(bf16[8,128,128]{2,1,0:T(8,128)(2,1)S(1)} %all-to-all-done.refs_0_), channel_id=1, source_target_pairs={{0,8},{8,0},{16,24},{24,16},{1,9},{9,1},{17,25},{25,17},{2,10},{10... | collective-permute-start | bytes 786440 | tf_op jit(solution)/shard_map/ppermute | solution.py:275
  68.3 5.9 %copy-start.4 = (bf16[8,128,128]{2,1,0:T(8,128)(2,1)}, bf16[8,128,128]{2,1,0:T(8,128)(2,1)S(1)}, u32[]{:S(2)}) copy-start(bf16[8,128,128]{2,1,0:T(8,128)(2,1)S(1)} %collective-permute-done.5.refs_5_) | copy-start | bytes 786436
  68.3 4.4 %collective-permute-start.7 = (bf16[8,128,128]{2,1,0:T(8,128)(2,1)S(1)}, bf16[8,128,128]{2,1,0:T(8,128)(2,1)S(1)}, u32[]{:S(2)}, u32[]{:S(2)}) collective-permute-start(bf16[8,128,128]{2,1,0:T(8,128)(2,1)S(1)} %collective-permute-done.5.refs_5_), channel_id=1, source_target_pairs={{0,8},{8,0},{16,24},{24,16},{1,9},{9,1},{17,25},{25,17},{2,10},{10... | collective-permute-start | bytes 786440 | tf_op jit(solution)/shard_map/ppermute | solution.py:275
  72.7 1.6 %copy-start.5 = (bf16[8,128,128]{2,1,0:T(8,128)(2,1)}, bf16[8,128,128]{2,1,0:T(8,128)(2,1)S(1)}, u32[]{:S(2)}) copy-start(bf16[8,128,128]{2,1,0:T(8,128)(2,1)S(1)} %collective-permute-done.4.refs_4_) | copy-start | bytes 786436
  72.7 1.5 %collective-permute-start.6 = (bf16[8,128,128]{2,1,0:T(8,128)(2,1)S(1)}, bf16[8,128,128]{2,1,0:T(8,128)(2,1)S(1)}, u32[]{:S(2)}, u32[]{:S(2)}) collective-permute-start(bf16[8,128,128]{2,1,0:T(8,128)(2,1)S(1)} %collective-permute-done.4.refs_4_), channel_id=1, source_target_pairs={{0,8},{8,0},{16,24},{24,16},{1,9},{9,1},{17,25},{25,17},{2,10},{10... | collective-permute-start | bytes 786440 | tf_op jit(solution)/shard_map/ppermute | solution.py:275
  72.7 1.6 %copy-start.6 = (bf16[8,128,128]{2,1,0:T(8,128)(2,1)}, bf16[8,128,128]{2,1,0:T(8,128)(2,1)S(1)}, u32[]{:S(2)}) copy-start(bf16[8,128,128]{2,1,0:T(8,128)(2,1)S(1)} %collective-permute-done.3.refs_3_) | copy-start | bytes 786436
  72.7 1.5 %copy-start.7 = (bf16[8,128,128]{2,1,0:T(8,128)(2,1)}, bf16[8,128,128]{2,1,0:T(8,128)(2,1)S(1)}, u32[]{:S(2)}) copy-start(bf16[8,128,128]{2,1,0:T(8,128)(2,1)S(1)} %collective-permute-done.2.refs_2_) | copy-start | bytes 786436
  72.7 1.5 %copy-start.8 = (bf16[8,128,128]{2,1,0:T(8,128)(2,1)}, bf16[8,128,128]{2,1,0:T(8,128)(2,1)S(1)}, u32[]{:S(2)}) copy-start(bf16[8,128,128]{2,1,0:T(8,128)(2,1)S(1)} %collective-permute-done.7.refs_7_) | copy-start | bytes 786436
  74.2 0.7 copy-start.9

commit v3 on v2

v3 whole, which is shorter than its diff:
```python
import functools

import jax
import jax.numpy as jnp
import numpy as np
from jax import lax
from jax.experimental import pallas as pl
from jax.experimental.pallas import tpu as pltpu
from jax.sharding import PartitionSpec as P

TRANSFORM = 8192
TAPS = 4
LANES = 128
SUB = 128
DEPTH = 512
PER_STEP = 2
CHUNK = 16
EDGE_DEPTH = 1024
EDGE_STEPS = 2
VMEM = 60 * 1024 * 1024
PIECES = 2


def prototype():
    sample = np.arange(TAPS * TRANSFORM, dtype=np.float64).reshape(TAPS, TRANSFORM)
    offset = (sample + 0.5) / TRANSFORM - TAPS / 2.0
    window = 0.5 - 0.5 * np.cos(2.0 * np.pi * (sample + 0.5) / (TAPS * TRANSFORM))
    return (np.sinc(offset) * window).astype(np.float32)


def fill_angles(kept, cos_held, sin_held, half=1):
    circle = 2 * TRANSFORM
    row = lax.broadcasted_iota(jnp.int32, cos_held.shape, 0)
    twice = jnp.where(row < SUB, 2 * row + half, 2 * SUB * (row - SUB))
    turns = jnp.bitwise_and(kept[...] * twice, circle - 1)
    angles = turns.astype(jnp.float32) * (2.0 * np.pi / circle)
    cos_held[...] = jnp.cos(angles)
    sin_held[...] = jnp.sin(angles)


def mix(spectra, parts, place, ahead, behind, out, mixed):
    slots, kept = len(spectra), spectra[0][0].shape[0]
    inside = jnp.where(place[0] == parts - 1, 0.0, 1.0)
    back = behind.shape[0]
    for s, values in enumerate(spectra):
        for p, value in enumerate(values):
            here = slice(p * kept, (p + 1) * kept)
            if s == 0:
                value = value + ahead[0, here].astype(jnp.float32)
            if s >= slots - back:
                value = value * inside + behind[s - (slots - back), here].astype(jnp.float32)
            for h in range(mixed.shape[0]):
                mixed[h, pl.ds(p * slots + s, kept, stride=2 * slots), :] = value[:, h * LANES : (h + 1) * LANES]
    rows = out.shape[1]
    for h in range(mixed.shape[0]):
        for i in range(out.shape[0]):
            out[i, :, h * LANES : (h + 1) * LANES] = mixed[h, i * rows : (i + 1) * rows, :].astype(out.dtype)


def dft_kernel(planes, frames, groups, extra, parts, *refs):
    nf, ng = len(frames), len(groups)
    ahead, mirror = refs[:nf], refs[nf : 2 * nf]
    coeff, channels, codes = refs[2 * nf : 2 * nf + 3]
    arrived, refs = refs[2 * nf + 3 : 2 * nf + 3 + extra], refs[2 * nf + 3 + extra :]
    outs, refs = refs[:ng], refs[ng:]
    mixed, refs = (refs[0], refs[1:]) if extra else (None, refs)
    cos_held, sin_held, acc_even, acc_odd = refs[:4]
    rows = ahead[0].shape[0]
    kept = channels.shape[1]
    step = pl.program_id(0)
    low = [p for p, (_, wanted) in enumerate(planes) if wanted]
    place = {p: (len(planes) + i) * rows for i, p in enumerate(low)}
    width = 2 * LANES
    span = DEPTH * PER_STEP
    backwards = LANES - 1 - lax.broadcasted_iota(jnp.int32, (CHUNK, LANES), 1)

    @pl.when(step == 0)
    def _():
        fill_angles(channels, cos_held, sin_held)
        acc_even[...] = jnp.zeros_like(acc_even)
        acc_odd[...] = jnp.zeros_like(acc_odd)

    for u in range(PER_STEP):
        even, odd, t_even, t_odd = refs[4 + 4 * u : 8 + 4 * u]
        for b in range(DEPTH // SUB):
            start = SUB + step * (span // SUB) + u * (DEPTH // SUB) + b
            for q in range(0, SUB, CHUNK):
                here = slice(b * SUB + q, b * SUB + q + CHUNK)
                cos_b, sin_b = cos_held[pl.ds(start, 1), :], sin_held[pl.ds(start, 1), :]
                cos_q, sin_q = cos_held[q : q + CHUNK, :], sin_held[q : q + CHUNK, :]
                for held, table in (
                    (t_even, cos_b * cos_q - sin_b * sin_q),
                    (t_odd, sin_b * cos_q + cos_b * sin_q),
                ):
                    high = table.astype(jnp.bfloat16)
                    held[here, :kept] = high
                    held[here, kept:] = (table - high.astype(jnp.float32)).astype(jnp.bfloat16)
        for w in range(0, DEPTH, width):
            at = u * DEPTH + w
            taps = [jnp.broadcast_to(coeff[t : t + 1, at : at + width], (CHUNK, width)) for t in range(TAPS)]
            for r in range(0, rows, CHUNK):
                fore, rear = {}, {}
                for i, f in enumerate(frames):
                    fore[f] = ahead[i][r : r + CHUNK, at : at + width].astype(jnp.float32)
                    seen = mirror[i][r : r + CHUNK, span - at - width : span - at].astype(jnp.float32)
                    rear[f] = jnp.concatenate(
                        [
                            jnp.take_along_axis(seen[:, c : c + LANES], backwards, axis=1)
                            for c in range(width - LANES, -1, -LANES)
                        ],
                        axis=1,
                    )
                for p, (s, _) in enumerate(planes):
                    x = z = None
                    for t in range(TAPS):
                        f = s - (TAPS - 1) + t
                        if f in fore:
                            a, b = taps[t] * fore[f], taps[TAPS - 1 - t] * rear[f]
                            x, z = (a, b) if x is None else (x + a, z + b)
                    for value, held in ((x + z, even), (x - z, odd)):
                        high = value.astype(jnp.bfloat16)
                        held[p * rows + r : p * rows + r + CHUNK, w : w + width] = high
                        if p in place:
                            rest = (value - high.astype(jnp.float32)).astype(jnp.bfloat16)
                            held[place[p] + r : place[p] + r + CHUNK, w : w + width] = rest
        acc_even[...] += jnp.dot(even[...], t_even[...], preferred_element_type=jnp.float32)
        acc_odd[...] += jnp.dot(odd[...], t_odd[...], preferred_element_type=jnp.float32)

    @pl.when(step == pl.num_programs(0) - 1)
    def _():
        def total(acc, p):
            value = acc[p * rows : (p + 1) * rows, :kept] + acc[p * rows : (p + 1) * rows, kept:]
            if p in place:
                rest = slice(place[p], place[p] + rows)
                value = value + acc[rest, :kept] + acc[rest, kept:]
            return value

        cos_h, sin_h = cos_held[0:1, :], sin_held[0:1, :]
        scale = codes[...].astype(jnp.float32) * (TRANSFORM**-0.5 / 16.0)
        def spectrum(p):
            even, odd = total(acc_even, p), total(acc_odd, p)
            return (cos_h * even + sin_h * odd).T * scale, (sin_h * even - cos_h * odd).T * scale

        if extra:
            mix([spectrum(p) for p in groups[0][0]], parts, *arrived[:3], outs[0], mixed)
        else:
            for out, (members, dtype) in zip(outs, groups):
                for i, p in enumerate(members):
                    out[i, :kept], out[i, kept:] = (v.astype(dtype) for v in spectrum(p))


def edge_kernel(planes, frames, groups, *refs):
    nf, ng = len(frames), len(groups)
    volts, (coeff, channels, codes) = refs[:nf], refs[nf : nf + 3]
    outs, (cos_held, sin_held, acc, *held) = refs[nf + 3 : nf + 3 + ng], refs[nf + 3 + ng :]
    rows, span = volts[0].shape
    kept = channels.shape[1]
    step = pl.program_id(0)
    width = 2 * LANES

    @pl.when(step == 0)
    def _():
        fill_angles(channels, cos_held, sin_held, 0)
        acc[...] = jnp.zeros_like(acc)

    for u in range(span // EDGE_DEPTH):
        filtered, table = held[2 * u : 2 * u + 2]
        for b in range(EDGE_DEPTH // SUB):
            start = SUB + step * (span // SUB) + u * (EDGE_DEPTH // SUB) + b
            for q in range(0, SUB, CHUNK):
                here = slice(b * SUB + q, b * SUB + q + CHUNK)
                cos_b, sin_b = cos_held[pl.ds(start, 1), :], sin_held[pl.ds(start, 1), :]
                cos_q, sin_q = cos_held[q : q + CHUNK, :], sin_held[q : q + CHUNK, :]
                table[here, :kept] = (cos_b * cos_q - sin_b * sin_q).astype(jnp.bfloat16)
                table[here, kept:] = (-sin_b * cos_q - cos_b * sin_q).astype(jnp.bfloat16)
        for w in range(0, EDGE_DEPTH, width):
            at = u * EDGE_DEPTH + w
            taps = [jnp.broadcast_to(coeff[t : t + 1, at : at + width], (CHUNK, width)) for t in range(TAPS)]
            for r in range(0, rows, CHUNK):
                seen = {
                    f: volts[i][r : r + CHUNK, at : at + width].astype(jnp.float32) for i, f in enumerate(frames)
                }
                for p, s in enumerate(planes):
                    terms = [taps[t] * seen[s - (TAPS - 1) + t] for t in range(TAPS) if s - (TAPS - 1) + t in seen]
                    filtered[p * rows + r : p * rows + r + CHUNK, w : w + width] = sum(terms[1:], terms[0]).astype(
                        jnp.bfloat16
                    )
        acc[...] += jnp.dot(filtered[...], table[...], preferred_element_type=jnp.float32)

    @pl.when(step == pl.num_programs(0) - 1)
    def _():
        scale = codes[...].astype(jnp.float32) * (TRANSFORM**-0.5 / 16.0)
        for out, members in zip(outs, groups):
            for i, p in enumerate(members):
                out[i] = (acc[p * rows : (p + 1) * rows, :].T * scale).astype(out.dtype)


def edges(voltages, coeffs, channels, codes, planes, groups):
    rows = voltages.shape[0]
    own = voltages.shape[1] // TRANSFORM
    kept = channels.shape[1]
    span = EDGE_DEPTH * EDGE_STEPS
    steps = TRANSFORM // span
    frames = sorted({s - (TAPS - 1) + t for s in planes for t in range(TAPS)} & set(range(own)))

    def frame(f):
        return pl.BlockSpec((rows, span), lambda j: (0, f * steps + j))

    outs = [jax.ShapeDtypeStruct((len(m), 2 * kept, rows), jnp.bfloat16) for m in groups]
    table = pltpu.VMEM((SUB + TRANSFORM // SUB, kept), jnp.float32)
    return pl.pallas_call(
        functools.partial(edge_kernel, planes, frames, groups),
        grid=(steps,),
        in_specs=[frame(f) for f in frames]
        + [pl.BlockSpec((TAPS, span), lambda j: (0, j)), pl.BlockSpec((1, kept), lambda j: (0, 0))]
        + [pl.BlockSpec((1, rows), lambda j: (0, 0))],
        out_specs=[pl.BlockSpec(o.shape, lambda j: (0, 0, 0)) for o in outs],
        out_shape=outs,
        scratch_shapes=[table, table, pltpu.VMEM((len(planes) * rows, 2 * kept), jnp.float32)]
        + [
            pltpu.VMEM((len(planes) * rows, EDGE_DEPTH), jnp.bfloat16),
            pltpu.VMEM((EDGE_DEPTH, 2 * kept), jnp.bfloat16),
        ]
        * EDGE_STEPS,
        compiler_params=pltpu.CompilerParams(vmem_limit_bytes=VMEM),
        cost_estimate=pl.CostEstimate(
            flops=4 * rows * TRANSFORM * kept * len(planes),
            bytes_accessed=len(frames) * rows * TRANSFORM * 2,
            transcendentals=0,
        ),
    )(*[voltages] * len(frames), coeffs, channels, codes)


def spectra(voltages, coeffs, channels, codes, planes, groups, piece=0, pieces=1, arrived=(), parts=1):
    rows = voltages.shape[0] // pieces
    own = voltages.shape[1] // TRANSFORM
    span = DEPTH * PER_STEP
    steps = TRANSFORM // 2 // span
    kept = channels.shape[1]
    columns = 2 * kept
    frames = sorted({s - (TAPS - 1) + t for s, _ in planes for t in range(TAPS)} & set(range(own)))
    count = len(planes) + sum(wanted for _, wanted in planes)

    def ahead(f):
        return pl.BlockSpec((rows, span), lambda j: (piece, 2 * f * steps + j))

    def mirror(f):
        return pl.BlockSpec((rows, span), lambda j: (piece, 2 * f * steps + 2 * steps - 1 - j))

    if arrived:
        outs = [jax.ShapeDtypeStruct((parts, columns * len(planes) // parts, rows), jnp.bfloat16)]
        held = [pltpu.VMEM((rows // LANES, len(planes) * columns, LANES), jnp.float32)]
        came = [pl.BlockSpec(memory_space=pltpu.SMEM)] + [
            pl.BlockSpec((x.shape[0], columns, rows), lambda j: (0, 0, piece)) for x in arrived[1:3]
        ]
        came += [pl.BlockSpec(memory_space=pl.ANY)] * len(arrived[3:])
    else:
        outs = [jax.ShapeDtypeStruct((len(m), columns, rows), d) for m, d in groups]
        held, came = [], []
    table = pltpu.VMEM((SUB + TRANSFORM // 2 // SUB, kept), jnp.float32)
    part = [
        pltpu.VMEM((count * rows, DEPTH), jnp.bfloat16),
        pltpu.VMEM((count * rows, DEPTH), jnp.bfloat16),
        pltpu.VMEM((DEPTH, columns), jnp.bfloat16),
        pltpu.VMEM((DEPTH, columns), jnp.bfloat16),
    ]
    return pl.pallas_call(
        functools.partial(dft_kernel, planes, frames, groups, len(came), parts),
        grid=(steps,),
        in_specs=[ahead(f) for f in frames]
        + [mirror(f) for f in frames]
        + [pl.BlockSpec((TAPS, span), lambda j: (0, j)), pl.BlockSpec((1, kept), lambda j: (0, 0))]
        + [pl.BlockSpec((1, rows), lambda j: (0, piece)), *came],
        out_specs=[pl.BlockSpec(o.shape, lambda j: (0, 0, 0)) for o in outs],
        out_shape=outs,
        scratch_shapes=[*held, table, table]
        + [pltpu.VMEM((count * rows, columns), jnp.float32)] * 2
        + part * PER_STEP,
        compiler_params=pltpu.CompilerParams(vmem_limit_bytes=VMEM),
        cost_estimate=pl.CostEstimate(
            flops=2 * rows * TRANSFORM * columns * count,
            bytes_accessed=len(frames) * rows * TRANSFORM * 2,
            transcendentals=0,
        ),
    )(*[voltages] * (2 * len(frames)), coeffs, channels, codes, *arrived)


def combine_kernel(parts, place, own, ahead, behind, out, mixed):
    kept = own.shape[1] // 2
    mix([(own[s, :kept], own[s, kept:]) for s in range(own.shape[0])], parts, place, ahead, behind, out, mixed)


def combined(parts, me, own, ahead, behind, piece):
    slots, columns, rows = own.shape
    block = columns * slots // parts

    def arriving(x):
        return pl.BlockSpec((x.shape[0], columns, rows), lambda j: (0, 0, piece))

    return pl.pallas_call(
        functools.partial(combine_kernel, parts),
        grid=(1,),
        in_specs=[pl.BlockSpec(memory_space=pltpu.SMEM), pl.BlockSpec(own.shape, lambda j: (0, 0, 0))]
        + [arriving(ahead), arriving(behind)],
        out_specs=pl.BlockSpec((parts, block, rows), lambda j: (0, 0, 0)),
        out_shape=jax.ShapeDtypeStruct((parts, block, rows), jnp.bfloat16),
        scratch_shapes=[pltpu.VMEM((rows // LANES, slots * columns, LANES), jnp.float32)],
        compiler_params=pltpu.CompilerParams(vmem_limit_bytes=VMEM),
    )(me, own, ahead, behind)


def correlate_kernel(half, pair, spectra_count, pieces, sets, groups, seat, *refs):
    out, buffer, sems = refs[-3:]
    wide = 2 * half
    tile = 16 // wide
    me = seat[0]

    def copy(channel, slot):
        return pltpu.make_async_copy(buffer.at[slot], out.at[:, channel], sems.at[slot])

    def gathered(tiles, take):
        return jnp.concatenate([jnp.concatenate([t[take] for t in p], axis=0) for p in tiles], axis=1)

    def turn(step, carry):
        for group in range(pair // tile):
            at = pl.multiple_of((step * pair + group * tile) * wide, 16)
            tiles = [
                [
                    [
                        refs[(m * pieces + p) * sets + k][i, pl.ds(at, 16), :].astype(jnp.float32)
                        for k in range(sets)
                        for i in range(refs[k].shape[0])
                    ]
                    for p in range(pieces)
                ]
                for m in range(groups)
            ]
            for h in range(tile):
                c = group * tile + h
                columns = [gathered(t, slice(h * wide, (h + 1) * wide)) for t in tiles]
                left = columns[0]
                bit = 1
                while bit < groups:
                    swap = (me // bit) % 2 == 1
                    columns = [jnp.where(swap, columns[q ^ bit], columns[q]) for q in range(groups)]
                    bit *= 2
                right = jnp.concatenate(columns, axis=1).astype(jnp.bfloat16)
                row = lax.broadcasted_iota(jnp.int32, left.shape, 0) % wide
                turned = jnp.where(row < half, pltpu.roll(left, left.shape[0] - half, 0), -pltpu.roll(left, half, 0))
                both = jnp.concatenate([left.T, turned.T], axis=0).astype(jnp.bfloat16)
                result = jnp.dot(both, right, preferred_element_type=jnp.float32) * (1.0 / spectra_count)

                @pl.when(step > 0)
                def _():
                    copy(step * pair + c, c).wait()

                buffer[c, 0], buffer[c, 1] = result[: left.shape[1]], result[left.shape[1] :]
                copy(step * pair + c, c).start()
        return carry

    turns = out.shape[1] // pair
    lax.fori_loop(0, turns, turn, 0)
    for c in range(pair):
        copy((turns - 1) * pair + c, c).wait()


def correlated(seat, seen, half, spectra_count):
    groups, pieces, sets = len(seen), len(seen[0]), len(seen[0][0])
    wide = 2 * half
    block = seen[0][0][0].shape[1]
    rows = sum(p[0].shape[2] for p in seen[0])
    channels = block // wide
    pair = min(channels, 4)
    arrays = [a for mask in seen for piece in mask for a in piece]
    return pl.pallas_call(
        functools.partial(correlate_kernel, half, pair, spectra_count, pieces, sets, groups),
        grid_spec=pltpu.PrefetchScalarGridSpec(
            num_scalar_prefetch=1,
            grid=(1,),
            in_specs=[pl.BlockSpec(a.shape, lambda j, seat: (0, 0, 0)) for a in arrays],
            out_specs=pl.BlockSpec(memory_space=pl.ANY),
            scratch_shapes=[
                pltpu.VMEM((pair, 2, rows, groups * rows), jnp.float32),
                pltpu.SemaphoreType.DMA((pair,)),
            ],
        ),
        out_shape=jax.ShapeDtypeStruct((2, channels, rows, groups * rows), jnp.float32),
        compiler_params=pltpu.CompilerParams(vmem_limit_bytes=VMEM),
        cost_estimate=pl.CostEstimate(
            flops=8 * spectra_count * rows * groups * rows * channels,
            bytes_accessed=2 * channels * rows * groups * rows * 4,
            transcendentals=0,
        ),
    )(seat, *arrays)


def exchanged(block, axis, mask):
    return lax.ppermute(block, axis, [(i, i ^ mask) for i in range(lax.axis_size(axis))])


def local(voltages, scale_codes, kept_channels):
    rows = voltages.shape[0]
    own = voltages.shape[1] // TRANSFORM
    history = TAPS - 1
    parts, groups = lax.axis_size("chan"), lax.axis_size("inp")
    me, seat = lax.axis_index("chan"), lax.axis_index("inp")
    coeffs = prototype()
    channels = kept_channels[None, :]
    codes = scale_codes[None, :]
    first = 2
    last = first + own
    edge = [*range(first), *range(last, own + history)]
    inner = [(s, s < last - 1) for s in range(first, last)]
    behind, ahead = edges(
        voltages, coeffs, channels, codes, edge, [list(range(first)), list(range(first, len(edge)))]
    )
    ahead = lax.ppermute(ahead, "chan", [(i, i + 1) for i in range(parts - 1)])
    behind = lax.ppermute(behind, "chan", [(i, (i - 1) % parts) for i in range(parts)])
    me, seat = me.astype(jnp.int32).reshape(1), seat.astype(jnp.int32).reshape(1)
    mine = []
    whole = [(list(range(own)), jnp.float32)]
    for piece in range(PIECES):
        if piece == 0:
            (planes,) = spectra(voltages, coeffs, channels, codes, inner, whole, piece, PIECES)
            blocks = combined(parts, me, planes, ahead, behind, piece)
        else:
            (blocks,) = spectra(
                voltages, coeffs, channels, codes, inner, whole, piece, PIECES, (me, ahead, behind, blocks), parts
            )
        mine.append([lax.all_to_all(blocks, "chan", 0, 0, tiled=True)])
    seen = {0: mine}
    bit = groups // 2
    while bit:
        seen.update({m | bit: [[exchanged(b, "inp", bit) for b in p] for p in seen[m]] for m in list(seen)})
        bit //= 2
    return correlated(seat, [seen[m] for m in range(groups)], own, own * parts)


def solution(mesh):
    placed = (P("inp", "chan"), P("inp"), P())
    return jax.shard_map(
        local, mesh=mesh, in_specs=placed, out_specs=P(None, "chan", "inp", None), check_vma=False
    )
```

time: 89.3 us -> 83.8 us (0.938)
  Pallas kernels: 52.3 us -> 48.5 us
  other arithmetic: 1.73 us -> 0 us
    pallas_call x2 -> x1, Pallas kernels: 3.92 us -> 1.98 us  [combined(): pl.pallas_call(functools.partial(combine_kernel, parts), grid=(1,), in_sp...]
    sin x1 -> x0, other arithmetic: 1.72 us -> none  [angle_tables(): return (jnp.cos(angles), jnp.sin(angles))]
    pallas_call x1, Pallas kernels: 14 us -> 13.1 us  [correlated(): pl.pallas_call(functools.partial(correlate_kernel, half, pair, spectra_co...]
    pallas_call x3, Pallas kernels: 34.4 us -> 33.5 us  [the longest x2 23.9 us: spectra(): pl.pallas_call(functools.partial(dft_kernel, planes, frames, groups, len(...]
where the time goes in v3:
time: 83.8 us; the launch traced here: 83.4 us
  Pallas kernels  48.5 us (58%)
  starting transfers between devices  20.8 us (25%)
  waiting for transfers between devices  12.5 us (15%)
  local copies, waits for them, and re-layouts  1.4 us (2%)
    pallas_call x2, Pallas kernels, spectra(): pl.pallas_call(functools.partial(dft_kernel, planes, frames, groups, len(...  23.9 us
    pallas_call x1, Pallas kernels, correlated(): pl.pallas_call(functools.partial(correlate_kernel, half, pair, spectra_co...  13.1 us
    all_to_all x2, starting transfers between devices, local(): mine.append([lax.all_to_all(blocks, 'chan', 0, 0, tiled=True)])  9.94 us
    pallas_call x1, Pallas kernels, edges(): pl.pallas_call(functools.partial(edge_kernel, planes, frames, groups), gr...  9.56 us
    all_to_all x2, waiting for transfers between devices, local(): mine.append([lax.all_to_all(blocks, 'chan', 0, 0, tiled=True)])  6.74 us
    ppermute x6, waiting for transfers between devices, exchanged(): lax.ppermute(block, axis, [(i, i ^ mask) for i in range(lax.axis_size(axi...  5.78 us
    ppermute x1, starting transfers between devices, local(): ahead = lax.ppermute(ahead, 'chan', [(i, i + 1) for i in range(parts - 1)])  4.87 us
    ppermute x6, starting transfers between devices, exchanged(): lax.ppermute(block, axis, [(i, i ^ mask) for i in range(lax.axis_size(axi...  3.56 us
  transfers between devices with their start and end apart: 10, of which 3 were waited for; matrix products, arithmetic and copies ran while one was open for 0% of the time, Pallas kernels for 29%

profile of v3, /device:TPU:0, one launch (start us, length us, event | category | flops | bytes accessed | tf_op | source)
XLA Modules:
  0.0 83.4 jit_solution(14824216058082033775)
XLA Ops:
  0.0 9.6 %shard_map.47 = (bf16[2,256,256]{2,1,0:T(8,128)(2,1)}, bf16[1,256,256]{2,1,0:T(8,128)(2,1)}) custom-call(bf16[256,32768]{1,0:T(8,128)(2,1)} %refs_7_.3, bf16[256,32768]{1,0:T(8,128)(2,1)} %refs_7_.3, bf16[256,32768]{1,0:T(8,128)(2,1)} %refs_7_.3, f32[4,8192]{1,0:T(4,128)} %constant.10.clone.refs_8_.refs_3_, s32[1,128]{1,0:T(1,128)} %bitcast.7, s32[1,256]{1,0:T(1,128)} %bitcast.4), custom_call_target="tpu_custom_call" | custom-call | flops 3221225472 | bytes 12582912 | tf_op jit(solution)/shard_map/pallas_call | solution.py:211
  9.6 4.9 %collective-permute-start = (bf16[1,256,256]{2,1,0:T(8,128)(2,1)}, bf16[1,256,256]{2,1,0:T(8,128)(2,1)S(1)}, u32[]{:S(2)}, u32[]{:S(2)}) collective-permute-start(bf16[1,256,256]{2,1,0:T(8,128)(2,1)} %get-tuple-element.7), channel_id=1, source_target_pairs={{0,1},{1,2},{2,3},{3,4},{4,5},{5,6},{6,7},{8,9},{9,10},{10,11},{11... | collective-permute-start | bytes 393224 | tf_op jit(solution)/shard_map/ppermute | solution.py:417
  14.4 2.5 %collective-permute-start.1 = (bf16[2,256,256]{2,1,0:T(8,128)(2,1)}, bf16[2,256,256]{2,1,0:T(8,128)(2,1)S(1)}, u32[]{:S(2)}, u32[]{:S(2)}) collective-permute-start(bf16[2,256,256]{2,1,0:T(8,128)(2,1)} %get-tuple-element.8), channel_id=1, source_target_pairs={{0,7},{1,0},{2,1},{3,2},{4,3},{5,4},{6,5},{7,6},{8,15},{9,8},{10,9... | collective-permute-start | bytes 786440 | tf_op jit(solution)/shard_map/ppermute | solution.py:418
  16.9 11.8 %shard_map.46.own = f32[4,256,128]{2,1,0:T(8,128)} custom-call(bf16[256,32768]{1,0:T(8,128)(2,1)} %refs_7_.3, bf16[256,32768]{1,0:T(8,128)(2,1)} %refs_7_.3, bf16[256,32768]{1,0:T(8,128)(2,1)} %refs_7_.3, bf16[256,32768]{1,0:T(8,128)(2,1)} %refs_7_.3, bf16[256,32768]{1,0:T(8,128)(2,1)} %refs_7_.3, bf16[256,32768]{1,0:T(8,128)(2,1)} %refs_7_.3, ...), custom_call_target="tpu_custom_call" | custom-call | flops 3758096384 | bytes 8388608 | tf_op jit(solution)/shard_map/pallas_call | solution.py:267
  28.7 0.0 collective-permute-done.ahead.refs_12_
  28.7 0.0 collective-permute-done.1.behind.refs_13_
  28.8 0.6 copy-done.3
  29.4 0.1 copy-done.2
  29.5 2.0 %shard_map.48.refs_14_ = bf16[8,128,128]{2,1,0:T(8,128)(2,1)} custom-call(s32[1]{0:T(128)} %bitcast.1.place.refs_11_, f32[4,256,128]{2,1,0:T(8,128)} %shard_map.46.own, bf16[1,256,256]{2,1,0:T(8,128)(2,1)} %copy-done.3, bf16[2,256,256]{2,1,0:T(8,128)(2,1)} %copy-done.2), custom_call_target="tpu_custom_call" | custom-call | tf_op jit(solution)/shard_map/pallas_call | solution.py:300
  31.5 3.9 %all-to-all-start = ((bf16[8,128,128]{2,1,0:T(8,128)(2,1)}), bf16[8,128,128]{2,1,0:T(8,128)(2,1)S(1)}, u32[]{:S(2)}, u32[]{:S(2)}) async-start(bf16[8,128,128]{2,1,0:T(8,128)(2,1)} %shard_map.48.refs_14_), calls=%async_computation | async-start | bytes 524288 | tf_op jit(solution)/shard_map/all_to_all | solution.py:430
  35.4 12.1 %shard_map.49 = bf16[8,128,128]{2,1,0:T(8,128)(2,1)} custom-call(bf16[256,32768]{1,0:T(8,128)(2,1)} %refs_7_.3, bf16[256,32768]{1,0:T(8,128)(2,1)} %refs_7_.3, bf16[256,32768]{1,0:T(8,128)(2,1)} %refs_7_.3, bf16[256,32768]{1,0:T(8,128)(2,1)} %refs_7_.3, bf16[256,32768]{1,0:T(8,128)(2,1)} %refs_7_.3, bf16[256,32768]{1,0:T(8,128)(2,1)} %refs_7_.3, ...), custom_call_target="tpu_custom_call" | custom-call | flops 3758096384 | bytes 8388608 | tf_op jit(solution)/shard_map/pallas_call | solution.py:267
  47.5 6.0 %all-to-all-start.1 = ((bf16[8,128,128]{2,1,0:T(8,128)(2,1)}), bf16[8,128,128]{2,1,0:T(8,128)(2,1)S(1)}, u32[]{:S(2)}, u32[]{:S(2)}) async-start(bf16[8,128,128]{2,1,0:T(8,128)(2,1)} %shard_map.49), calls=%async_computation.1 | async-start | bytes 524288 | tf_op jit(solution)/shard_map/all_to_all | solution.py:430
  53.5 1.5 %collective-permute-start.4 = (bf16[8,128,128]{2,1,0:T(8,128)(2,1)S(1)}, bf16[8,128,128]{2,1,0:T(8,128)(2,1)S(1)}, u32[]{:S(2)}, u32[]{:S(2)}) collective-permute-start(bf16[8,128,128]{2,1,0:T(8,128)(2,1)S(1)} %all-to-all-done.refs_0_), channel_id=1, source_target_pairs={{0,16},{8,24},{16,0},{24,8},{1,17},{9,25},{17,1},{25,9},{2,18},{10... | collective-permute-start | bytes 786440 | tf_op jit(solution)/shard_map/ppermute | solution.py:398
  55.0 6.7 %all-to-all-done.1.refs_1_ = bf16[8,128,128]{2,1,0:T(8,128)(2,1)S(1)} async-done(((bf16[8,128,128]{2,1,0:T(8,128)(2,1)}), bf16[8,128,128]{2,1,0:T(8,128)(2,1)S(1)}, u32[]{:S(2)}, u32[]{:S(2)}) %all-to-all-start.1) | async-done | bytes 262176 | tf_op jit(solution)/shard_map/all_to_all | solution.py:430
  61.7 1.5 %collective-permute-start.5 = (bf16[8,128,128]{2,1,0:T(8,128)(2,1)S(1)}, bf16[8,128,128]{2,1,0:T(8,128)(2,1)S(1)}, u32[]{:S(2)}, u32[]{:S(2)}) collective-permute-start(bf16[8,128,128]{2,1,0:T(8,128)(2,1)S(1)} %all-to-all-done.1.refs_1_), channel_id=1, source_target_pairs={{0,16},{8,24},{16,0},{24,8},{1,17},{9,25},{17,1},{25,9},{2,18},{10... | collective-permute-start | bytes 786440 | tf_op jit(solution)/shard_map/ppermute | solution.py:398
  63.2 0.5 collective-permute-start.3
  63.8 0.0 collective-permute-done.4.refs_4_
  63.8 0.1 collective-permute-start.6
  63.8 4.3 %collective-permute-done.5.refs_5_ = bf16[8,128,128]{2,1,0:T(8,128)(2,1)S(1)} collective-permute-done((bf16[8,128,128]{2,1,0:T(8,128)(2,1)S(1)}, bf16[8,128,128]{2,1,0:T(8,128)(2,1)S(1)}, u32[]{:S(2)}, u32[]{:S(2)}) %collective-permute-start.5) | collective-permute-done | bytes 262176 | tf_op jit(solution)/shard_map/ppermute | solution.py:398
  68.1 0.0 collective-permute-done.3.refs_3_
  68.2 0.0 collective-permute-done.6.refs_6_
  68.2 1.5 %collective-permute-done.7.refs_7_ = bf16[8,128,128]{2,1,0:T(8,128)(2,1)S(1)} collective-permute-done((bf16[8,128,128]{2,1,0:T(8,128)(2,1)S(1)}, bf16[8,128,128]{2,1,0:T(8,128)(2,1)S(1)}, u32[]{:S(2)}, u32[]{:S(2)}) %collective-permute-start.7) | collective-permute-done | bytes 262176 | tf_op jit(solution)/shard_map/ppermute | solution.py:398
  69.7 0.6 copy-done.9
  70.4 13.1 %shard_map.50 = f32[2,16,256,1024]{3,2,1,0:T(8,128)} custom-call(s32[1]{0:T(128)} %bitcast.seat, bf16[8,128,128]{2,1,0:T(8,128)(2,1)} %copy-done, bf16[8,128,128]{2,1,0:T(8,128)(2,1)} %copy-done.1, bf16[8,128,128]{2,1,0:T(8,128)(2,1)} %copy-done.6, bf16[8,128,128]{2,1,0:T(8,128)(2,1)} %copy-done.7, bf16[8,128,128]{2,1,0:T(8,128)(2,1)} %copy-done.4, ...), custom_call_target="tpu_custom_call" | custom-call | flops 1073741824 | bytes 33554432 | tf_op jit(solution)/shard_map/pallas_call | solution.py:375
  (21 shorter events, 0.0 us)
Async XLA Ops:
  9.6 19.2 %collective-permute-start = (bf16[1,256,256]{2,1,0:T(8,128)(2,1)}, bf16[1,256,256]{2,1,0:T(8,128)(2,1)S(1)}, u32[]{:S(2)}, u32[]{:S(2)}) collective-permute-start(bf16[1,256,256]{2,1,0:T(8,128)(2,1)} %get-tuple-element.7), channel_id=1, source_target_pairs={{0,1},{1,2},{2,3},{3,4},{4,5},{5,6},{6,7},{8,9},{9,10},{10,11},{11... | collective-permute-start | bytes 393224 | tf_op jit(solution)/shard_map/ppermute | solution.py:417
  14.4 14.3 %collective-permute-start.1 = (bf16[2,256,256]{2,1,0:T(8,128)(2,1)}, bf16[2,256,256]{2,1,0:T(8,128)(2,1)S(1)}, u32[]{:S(2)}, u32[]{:S(2)}) collective-permute-start(bf16[2,256,256]{2,1,0:T(8,128)(2,1)} %get-tuple-element.8), channel_id=1, source_target_pairs={{0,7},{1,0},{2,1},{3,2},{4,3},{5,4},{6,5},{7,6},{8,15},{9,8},{10,9... | collective-permute-start | bytes 786440 | tf_op jit(solution)/shard_map/ppermute | solution.py:418
  28.7 0.7 copy-start.3
  28.7 0.7 copy-start.2
  31.5 16.0 %all-to-all-start = ((bf16[8,128,128]{2,1,0:T(8,128)(2,1)}), bf16[8,128,128]{2,1,0:T(8,128)(2,1)S(1)}, u32[]{:S(2)}, u32[]{:S(2)}) async-start(bf16[8,128,128]{2,1,0:T(8,128)(2,1)} %shard_map.48.refs_14_), calls=%async_computation | async-start | bytes 524288 | tf_op jit(solution)/shard_map/all_to_all | solution.py:430
  47.5 22.2 %copy-start = (bf16[8,128,128]{2,1,0:T(8,128)(2,1)}, bf16[8,128,128]{2,1,0:T(8,128)(2,1)S(1)}, u32[]{:S(2)}) copy-start(bf16[8,128,128]{2,1,0:T(8,128)(2,1)S(1)} %all-to-all-done.refs_0_) | copy-start | bytes 786436
  47.5 14.2 %all-to-all-start.1 = ((bf16[8,128,128]{2,1,0:T(8,128)(2,1)}), bf16[8,128,128]{2,1,0:T(8,128)(2,1)S(1)}, u32[]{:S(2)}, u32[]{:S(2)}) async-start(bf16[8,128,128]{2,1,0:T(8,128)(2,1)} %shard_map.49), calls=%async_computation.1 | async-start | bytes 524288 | tf_op jit(solution)/shard_map/all_to_all | solution.py:430
  53.5 10.2 %collective-permute-start.4 = (bf16[8,128,128]{2,1,0:T(8,128)(2,1)S(1)}, bf16[8,128,128]{2,1,0:T(8,128)(2,1)S(1)}, u32[]{:S(2)}, u32[]{:S(2)}) collective-permute-start(bf16[8,128,128]{2,1,0:T(8,128)(2,1)S(1)} %all-to-all-done.refs_0_), channel_id=1, source_target_pairs={{0,16},{8,24},{16,0},{24,8},{1,17},{9,25},{17,1},{25,9},{2,18},{10... | collective-permute-start | bytes 786440 | tf_op jit(solution)/shard_map/ppermute | solution.py:398
  61.7 7.9 %copy-start.1 = (bf16[8,128,128]{2,1,0:T(8,128)(2,1)}, bf16[8,128,128]{2,1,0:T(8,128)(2,1)S(1)}, u32[]{:S(2)}) copy-start(bf16[8,128,128]{2,1,0:T(8,128)(2,1)S(1)} %all-to-all-done.1.refs_1_) | copy-start | bytes 786436
  61.7 6.4 %collective-permute-start.5 = (bf16[8,128,128]{2,1,0:T(8,128)(2,1)S(1)}, bf16[8,128,128]{2,1,0:T(8,128)(2,1)S(1)}, u32[]{:S(2)}, u32[]{:S(2)}) collective-permute-start(bf16[8,128,128]{2,1,0:T(8,128)(2,1)S(1)} %all-to-all-done.1.refs_1_), channel_id=1, source_target_pairs={{0,16},{8,24},{16,0},{24,8},{1,17},{9,25},{17,1},{25,9},{2,18},{10... | collective-permute-start | bytes 786440 | tf_op jit(solution)/shard_map/ppermute | solution.py:398
  63.2 4.9 %collective-permute-start.2 = (bf16[8,128,128]{2,1,0:T(8,128)(2,1)S(1)}, bf16[8,128,128]{2,1,0:T(8,128)(2,1)S(1)}, u32[]{:S(2)}, u32[]{:S(2)}) collective-permute-start(bf16[8,128,128]{2,1,0:T(8,128)(2,1)S(1)} %all-to-all-done.refs_0_), channel_id=1, source_target_pairs={{0,8},{8,0},{16,24},{24,16},{1,9},{9,1},{17,25},{25,17},{2,10},{10... | collective-permute-start | bytes 786440 | tf_op jit(solution)/shard_map/ppermute | solution.py:398
  63.2 4.9 %collective-permute-start.3 = (bf16[8,128,128]{2,1,0:T(8,128)(2,1)S(1)}, bf16[8,128,128]{2,1,0:T(8,128)(2,1)S(1)}, u32[]{:S(2)}, u32[]{:S(2)}) collective-permute-start(bf16[8,128,128]{2,1,0:T(8,128)(2,1)S(1)} %all-to-all-done.1.refs_1_), channel_id=1, source_target_pairs={{0,8},{8,0},{16,24},{24,16},{1,9},{9,1},{17,25},{25,17},{2,10},{10... | collective-permute-start | bytes 786440 | tf_op jit(solution)/shard_map/ppermute | solution.py:398
  63.8 5.9 %copy-start.4 = (bf16[8,128,128]{2,1,0:T(8,128)(2,1)}, bf16[8,128,128]{2,1,0:T(8,128)(2,1)S(1)}, u32[]{:S(2)}) copy-start(bf16[8,128,128]{2,1,0:T(8,128)(2,1)S(1)} %collective-permute-done.4.refs_4_) | copy-start | bytes 786436
  63.8 4.4 %collective-permute-start.6 = (bf16[8,128,128]{2,1,0:T(8,128)(2,1)S(1)}, bf16[8,128,128]{2,1,0:T(8,128)(2,1)S(1)}, u32[]{:S(2)}, u32[]{:S(2)}) collective-permute-start(bf16[8,128,128]{2,1,0:T(8,128)(2,1)S(1)} %collective-permute-done.4.refs_4_), channel_id=1, source_target_pairs={{0,8},{8,0},{16,24},{24,16},{1,9},{9,1},{17,25},{25,17},{2,10},{10... | collective-permute-start | bytes 786440 | tf_op jit(solution)/shard_map/ppermute | solution.py:398
  68.1 1.6 %copy-start.5 = (bf16[8,128,128]{2,1,0:T(8,128)(2,1)}, bf16[8,128,128]{2,1,0:T(8,128)(2,1)S(1)}, u32[]{:S(2)}) copy-start(bf16[8,128,128]{2,1,0:T(8,128)(2,1)S(1)} %collective-permute-done.5.refs_5_) | copy-start | bytes 786436
  68.1 1.5 %collective-permute-start.7 = (bf16[8,128,128]{2,1,0:T(8,128)(2,1)S(1)}, bf16[8,128,128]{2,1,0:T(8,128)(2,1)S(1)}, u32[]{:S(2)}, u32[]{:S(2)}) collective-permute-start(bf16[8,128,128]{2,1,0:T(8,128)(2,1)S(1)} %collective-permute-done.5.refs_5_), channel_id=1, source_target_pairs={{0,8},{8,0},{16,24},{24,16},{1,9},{9,1},{17,25},{25,17},{2,10},{10... | collective-permute-start | bytes 786440 | tf_op jit(solution)/shard_map/ppermute | solution.py:398
  68.1 1.6 %copy-start.6 = (bf16[8,128,128]{2,1,0:T(8,128)(2,1)}, bf16[8,128,128]{2,1,0:T(8,128)(2,1)S(1)}, u32[]{:S(2)}) copy-start(bf16[8,128,128]{2,1,0:T(8,128)(2,1)S(1)} %collective-permute-done.2.refs_2_) | copy-start | bytes 786436
  68.2 1.5 %copy-start.7 = (bf16[8,128,128]{2,1,0:T(8,128)(2,1)}, bf16[8,128,128]{2,1,0:T(8,128)(2,1)S(1)}, u32[]{:S(2)}) copy-start(bf16[8,128,128]{2,1,0:T(8,128)(2,1)S(1)} %collective-permute-done.3.refs_3_) | copy-start | bytes 786436
  68.2 1.5 %copy-start.8 = (bf16[8,128,128]{2,1,0:T(8,128)(2,1)}, bf16[8,128,128]{2,1,0:T(8,128)(2,1)S(1)}, u32[]{:S(2)}) copy-start(bf16[8,128,128]{2,1,0:T(8,128)(2,1)S(1)} %collective-permute-done.6.refs_6_) | copy-start | bytes 786436
  69.7 0.7 copy-start.9

commit v4 on v3

--- a/solution.py
+++ b/solution.py
@@ -15,6 +15,7 @@
 DEPTH = 512
 PER_STEP = 2
 CHUNK = 16
+EDGE_CHUNK = 32
 EDGE_DEPTH = 1024
 EDGE_STEPS = 2
 VMEM = 60 * 1024 * 1024
@@ -70,7 +71,7 @@
     step = pl.program_id(0)
     low = [p for p, (_, wanted) in enumerate(planes) if wanted]
     place = {p: (len(planes) + i) * rows for i, p in enumerate(low)}
-    width = 2 * LANES
+    width = 4 * LANES
     span = DEPTH * PER_STEP
     backwards = LANES - 1 - lax.broadcasted_iota(jnp.int32, (CHUNK, LANES), 1)
 
@@ -167,22 +168,22 @@
         filtered, table = held[2 * u : 2 * u + 2]
         for b in range(EDGE_DEPTH // SUB):
             start = SUB + step * (span // SUB) + u * (EDGE_DEPTH // SUB) + b
-            for q in range(0, SUB, CHUNK):
-                here = slice(b * SUB + q, b * SUB + q + CHUNK)
+            for q in range(0, SUB, EDGE_CHUNK):
+                here = slice(b * SUB + q, b * SUB + q + EDGE_CHUNK)
                 cos_b, sin_b = cos_held[pl.ds(start, 1), :], sin_held[pl.ds(start, 1), :]
-                cos_q, sin_q = cos_held[q : q + CHUNK, :], sin_held[q : q + CHUNK, :]
+                cos_q, sin_q = cos_held[q : q + EDGE_CHUNK, :], sin_held[q : q + EDGE_CHUNK, :]
                 table[here, :kept] = (cos_b * cos_q - sin_b * sin_q).astype(jnp.bfloat16)
                 table[here, kept:] = (-sin_b * cos_q - cos_b * sin_q).astype(jnp.bfloat16)
         for w in range(0, EDGE_DEPTH, width):
             at = u * EDGE_DEPTH + w
-            taps = [jnp.broadcast_to(coeff[t : t + 1, at : at + width], (CHUNK, width)) for t in range(TAPS)]
-            for r in range(0, rows, CHUNK):
+            taps = [jnp.broadcast_to(coeff[t : t + 1, at : at + width], (EDGE_CHUNK, width)) for t in range(TAPS)]
+            for r in range(0, rows, EDGE_CHUNK):
                 seen = {
-                    f: volts[i][r : r + CHUNK, at : at + width].astype(jnp.float32) for i, f in enumerate(frames)
+                    f: volts[i][r : r + EDGE_CHUNK, at : at + width].astype(jnp.float32) for i, f in enumerate(frames)
                 }
                 for p, s in enumerate(planes):
                     terms = [taps[t] * seen[s - (TAPS - 1) + t] for t in range(TAPS) if s - (TAPS - 1) + t in seen]
-                    filtered[p * rows + r : p * rows + r + CHUNK, w : w + width] = sum(terms[1:], terms[0]).astype(
+                    filtered[p * rows + r : p * rows + r + EDGE_CHUNK, w : w + width] = sum(terms[1:], terms[0]).astype(
                         jnp.bfloat16
                     )
         acc[...] += jnp.dot(filtered[...], table[...], preferred_element_type=jnp.float32)

time: 83.8 us -> 83.8 us (level)
  no operation moved by 1% of the time
where the time goes in v4:
time: 83.8 us; the launch traced here: 83.4 us
  Pallas kernels  48.5 us (58%)
  starting transfers between devices  20.8 us (25%)
  waiting for transfers between devices  12.5 us (15%)
  local copies, waits for them, and re-layouts  1.4 us (2%)
    pallas_call x2, Pallas kernels, spectra(): pl.pallas_call(functools.partial(dft_kernel, planes, frames, groups, len(...  23.9 us
    pallas_call x1, Pallas kernels, correlated(): pl.pallas_call(functools.partial(correlate_kernel, half, pair, spectra_co...  13 us
    all_to_all x2, starting transfers between devices, local(): mine.append([lax.all_to_all(blocks, 'chan', 0, 0, tiled=True)])  9.94 us
    pallas_call x1, Pallas kernels, edges(): pl.pallas_call(functools.partial(edge_kernel, planes, frames, groups), gr...  9.56 us
    all_to_all x2, waiting for transfers between devices, local(): mine.append([lax.all_to_all(blocks, 'chan', 0, 0, tiled=True)])  6.74 us
    ppermute x6, waiting for transfers between devices, exchanged(): lax.ppermute(block, axis, [(i, i ^ mask) for i in range(lax.axis_size(axi...  5.78 us
    ppermute x1, starting transfers between devices, local(): ahead = lax.ppermute(ahead, 'chan', [(i, i + 1) for i in range(parts - 1)])  4.87 us
    ppermute x6, starting transfers between devices, exchanged(): lax.ppermute(block, axis, [(i, i ^ mask) for i in range(lax.axis_size(axi...  3.56 us
  transfers between devices with their start and end apart: 10, of which 3 were waited for; matrix products, arithmetic and copies ran while one was open for 0% of the time, Pallas kernels for 29%

profile of v4, /device:TPU:0, one launch (start us, length us, event | category | flops | bytes accessed | tf_op | source)
XLA Modules:
  0.0 83.4 jit_solution(14380741577551965064)
XLA Ops:
  0.0 9.6 %shard_map.47 = (bf16[2,256,256]{2,1,0:T(8,128)(2,1)}, bf16[1,256,256]{2,1,0:T(8,128)(2,1)}) custom-call(bf16[256,32768]{1,0:T(8,128)(2,1)} %refs_7_.3, bf16[256,32768]{1,0:T(8,128)(2,1)} %refs_7_.3, bf16[256,32768]{1,0:T(8,128)(2,1)} %refs_7_.3, f32[4,8192]{1,0:T(4,128)} %constant.10.clone.refs_8_.refs_3_, s32[1,128]{1,0:T(1,128)} %bitcast.7, s32[1,256]{1,0:T(1,128)} %bitcast.4), custom_call_target="tpu_custom_call" | custom-call | flops 3221225472 | bytes 12582912 | tf_op jit(solution)/shard_map/pallas_call | solution.py:212
  9.6 4.9 %collective-permute-start = (bf16[1,256,256]{2,1,0:T(8,128)(2,1)}, bf16[1,256,256]{2,1,0:T(8,128)(2,1)S(1)}, u32[]{:S(2)}, u32[]{:S(2)}) collective-permute-start(bf16[1,256,256]{2,1,0:T(8,128)(2,1)} %get-tuple-element.7), channel_id=1, source_target_pairs={{0,1},{1,2},{2,3},{3,4},{4,5},{5,6},{6,7},{8,9},{9,10},{10,11},{11... | collective-permute-start | bytes 393224 | tf_op jit(solution)/shard_map/ppermute | solution.py:418
  14.4 2.5 %collective-permute-start.1 = (bf16[2,256,256]{2,1,0:T(8,128)(2,1)}, bf16[2,256,256]{2,1,0:T(8,128)(2,1)S(1)}, u32[]{:S(2)}, u32[]{:S(2)}) collective-permute-start(bf16[2,256,256]{2,1,0:T(8,128)(2,1)} %get-tuple-element.8), channel_id=1, source_target_pairs={{0,7},{1,0},{2,1},{3,2},{4,3},{5,4},{6,5},{7,6},{8,15},{9,8},{10,9... | collective-permute-start | bytes 786440 | tf_op jit(solution)/shard_map/ppermute | solution.py:419
  16.9 11.8 %shard_map.46.own = f32[4,256,128]{2,1,0:T(8,128)} custom-call(bf16[256,32768]{1,0:T(8,128)(2,1)} %refs_7_.3, bf16[256,32768]{1,0:T(8,128)(2,1)} %refs_7_.3, bf16[256,32768]{1,0:T(8,128)(2,1)} %refs_7_.3, bf16[256,32768]{1,0:T(8,128)(2,1)} %refs_7_.3, bf16[256,32768]{1,0:T(8,128)(2,1)} %refs_7_.3, bf16[256,32768]{1,0:T(8,128)(2,1)} %refs_7_.3, ...), custom_call_target="tpu_custom_call" | custom-call | flops 3758096384 | bytes 8388608 | tf_op jit(solution)/shard_map/pallas_call | solution.py:268
  28.7 0.0 collective-permute-done.1.behind.refs_13_
  28.7 0.6 copy-done.3
  29.4 0.1 copy-done.2
  29.5 2.0 %shard_map.48.refs_14_ = bf16[8,128,128]{2,1,0:T(8,128)(2,1)} custom-call(s32[1]{0:T(128)} %bitcast.1.place.refs_11_, f32[4,256,128]{2,1,0:T(8,128)} %shard_map.46.own, bf16[1,256,256]{2,1,0:T(8,128)(2,1)} %copy-done.3, bf16[2,256,256]{2,1,0:T(8,128)(2,1)} %copy-done.2), custom_call_target="tpu_custom_call" | custom-call | tf_op jit(solution)/shard_map/pallas_call | solution.py:301
  31.5 3.9 %all-to-all-start = ((bf16[8,128,128]{2,1,0:T(8,128)(2,1)}), bf16[8,128,128]{2,1,0:T(8,128)(2,1)S(1)}, u32[]{:S(2)}, u32[]{:S(2)}) async-start(bf16[8,128,128]{2,1,0:T(8,128)(2,1)} %shard_map.48.refs_14_), calls=%async_computation | async-start | bytes 524288 | tf_op jit(solution)/shard_map/all_to_all | solution.py:431
  35.4 12.1 %shard_map.49 = bf16[8,128,128]{2,1,0:T(8,128)(2,1)} custom-call(bf16[256,32768]{1,0:T(8,128)(2,1)} %refs_7_.3, bf16[256,32768]{1,0:T(8,128)(2,1)} %refs_7_.3, bf16[256,32768]{1,0:T(8,128)(2,1)} %refs_7_.3, bf16[256,32768]{1,0:T(8,128)(2,1)} %refs_7_.3, bf16[256,32768]{1,0:T(8,128)(2,1)} %refs_7_.3, bf16[256,32768]{1,0:T(8,128)(2,1)} %refs_7_.3, ...), custom_call_target="tpu_custom_call" | custom-call | flops 3758096384 | bytes 8388608 | tf_op jit(solution)/shard_map/pallas_call | solution.py:268
  47.5 0.0 all-to-all-done.refs_0_
  47.5 6.0 %all-to-all-start.1 = ((bf16[8,128,128]{2,1,0:T(8,128)(2,1)}), bf16[8,128,128]{2,1,0:T(8,128)(2,1)S(1)}, u32[]{:S(2)}, u32[]{:S(2)}) async-start(bf16[8,128,128]{2,1,0:T(8,128)(2,1)} %shard_map.49), calls=%async_computation.1 | async-start | bytes 524288 | tf_op jit(solution)/shard_map/all_to_all | solution.py:431
  53.5 1.5 %collective-permute-start.4 = (bf16[8,128,128]{2,1,0:T(8,128)(2,1)S(1)}, bf16[8,128,128]{2,1,0:T(8,128)(2,1)S(1)}, u32[]{:S(2)}, u32[]{:S(2)}) collective-permute-start(bf16[8,128,128]{2,1,0:T(8,128)(2,1)S(1)} %all-to-all-done.refs_0_), channel_id=1, source_target_pairs={{0,16},{8,24},{16,0},{24,8},{1,17},{9,25},{17,1},{25,9},{2,18},{10... | collective-permute-start | bytes 786440 | tf_op jit(solution)/shard_map/ppermute | solution.py:399
  55.0 6.7 %all-to-all-done.1.refs_1_ = bf16[8,128,128]{2,1,0:T(8,128)(2,1)S(1)} async-done(((bf16[8,128,128]{2,1,0:T(8,128)(2,1)}), bf16[8,128,128]{2,1,0:T(8,128)(2,1)S(1)}, u32[]{:S(2)}, u32[]{:S(2)}) %all-to-all-start.1) | async-done | bytes 262176 | tf_op jit(solution)/shard_map/all_to_all | solution.py:431
  61.7 1.5 %collective-permute-start.5 = (bf16[8,128,128]{2,1,0:T(8,128)(2,1)S(1)}, bf16[8,128,128]{2,1,0:T(8,128)(2,1)S(1)}, u32[]{:S(2)}, u32[]{:S(2)}) collective-permute-start(bf16[8,128,128]{2,1,0:T(8,128)(2,1)S(1)} %all-to-all-done.1.refs_1_), channel_id=1, source_target_pairs={{0,16},{8,24},{16,0},{24,8},{1,17},{9,25},{17,1},{25,9},{2,18},{10... | collective-permute-start | bytes 786440 | tf_op jit(solution)/shard_map/ppermute | solution.py:399
  63.2 0.0 collective-permute-start.2
  63.2 0.5 collective-permute-start.3
  63.7 0.0 collective-permute-done.4.refs_4_
  63.7 0.1 collective-permute-start.6
  63.8 4.3 %collective-permute-done.5.refs_5_ = bf16[8,128,128]{2,1,0:T(8,128)(2,1)S(1)} collective-permute-done((bf16[8,128,128]{2,1,0:T(8,128)(2,1)S(1)}, bf16[8,128,128]{2,1,0:T(8,128)(2,1)S(1)}, u32[]{:S(2)}, u32[]{:S(2)}) %collective-permute-start.5) | collective-permute-done | bytes 262176 | tf_op jit(solution)/shard_map/ppermute | solution.py:399
  68.1 0.0 collective-permute-done.3.refs_3_
  68.2 1.5 %collective-permute-done.7.refs_7_ = bf16[8,128,128]{2,1,0:T(8,128)(2,1)S(1)} collective-permute-done((bf16[8,128,128]{2,1,0:T(8,128)(2,1)S(1)}, bf16[8,128,128]{2,1,0:T(8,128)(2,1)S(1)}, u32[]{:S(2)}, u32[]{:S(2)}) %collective-permute-start.7) | collective-permute-done | bytes 262176 | tf_op jit(solution)/shard_map/ppermute | solution.py:399
  69.7 0.6 copy-done.9
  70.3 13.0 %shard_map.50 = f32[2,16,256,1024]{3,2,1,0:T(8,128)} custom-call(s32[1]{0:T(128)} %bitcast.seat, bf16[8,128,128]{2,1,0:T(8,128)(2,1)} %copy-done, bf16[8,128,128]{2,1,0:T(8,128)(2,1)} %copy-done.1, bf16[8,128,128]{2,1,0:T(8,128)(2,1)} %copy-done.6, bf16[8,128,128]{2,1,0:T(8,128)(2,1)} %copy-done.7, bf16[8,128,128]{2,1,0:T(8,128)(2,1)} %copy-done.4, ...), custom_call_target="tpu_custom_call" | custom-call | flops 1073741824 | bytes 33554432 | tf_op jit(solution)/shard_map/pallas_call | solution.py:376
  (21 shorter events, 0.0 us)
Async XLA Ops:
  9.6 19.2 %collective-permute-start = (bf16[1,256,256]{2,1,0:T(8,128)(2,1)}, bf16[1,256,256]{2,1,0:T(8,128)(2,1)S(1)}, u32[]{:S(2)}, u32[]{:S(2)}) collective-permute-start(bf16[1,256,256]{2,1,0:T(8,128)(2,1)} %get-tuple-element.7), channel_id=1, source_target_pairs={{0,1},{1,2},{2,3},{3,4},{4,5},{5,6},{6,7},{8,9},{9,10},{10,11},{11... | collective-permute-start | bytes 393224 | tf_op jit(solution)/shard_map/ppermute | solution.py:418
  14.4 14.3 %collective-permute-start.1 = (bf16[2,256,256]{2,1,0:T(8,128)(2,1)}, bf16[2,256,256]{2,1,0:T(8,128)(2,1)S(1)}, u32[]{:S(2)}, u32[]{:S(2)}) collective-permute-start(bf16[2,256,256]{2,1,0:T(8,128)(2,1)} %get-tuple-element.8), channel_id=1, source_target_pairs={{0,7},{1,0},{2,1},{3,2},{4,3},{5,4},{6,5},{7,6},{8,15},{9,8},{10,9... | collective-permute-start | bytes 786440 | tf_op jit(solution)/shard_map/ppermute | solution.py:419
  28.7 0.7 copy-start.3
  28.7 0.7 copy-start.2
  31.5 16.0 %all-to-all-start = ((bf16[8,128,128]{2,1,0:T(8,128)(2,1)}), bf16[8,128,128]{2,1,0:T(8,128)(2,1)S(1)}, u32[]{:S(2)}, u32[]{:S(2)}) async-start(bf16[8,128,128]{2,1,0:T(8,128)(2,1)} %shard_map.48.refs_14_), calls=%async_computation | async-start | bytes 524288 | tf_op jit(solution)/shard_map/all_to_all | solution.py:431
  47.5 22.2 %copy-start = (bf16[8,128,128]{2,1,0:T(8,128)(2,1)}, bf16[8,128,128]{2,1,0:T(8,128)(2,1)S(1)}, u32[]{:S(2)}) copy-start(bf16[8,128,128]{2,1,0:T(8,128)(2,1)S(1)} %all-to-all-done.refs_0_) | copy-start | bytes 786436
  47.5 14.2 %all-to-all-start.1 = ((bf16[8,128,128]{2,1,0:T(8,128)(2,1)}), bf16[8,128,128]{2,1,0:T(8,128)(2,1)S(1)}, u32[]{:S(2)}, u32[]{:S(2)}) async-start(bf16[8,128,128]{2,1,0:T(8,128)(2,1)} %shard_map.49), calls=%async_computation.1 | async-start | bytes 524288 | tf_op jit(solution)/shard_map/all_to_all | solution.py:431
  53.5 10.2 %collective-permute-start.4 = (bf16[8,128,128]{2,1,0:T(8,128)(2,1)S(1)}, bf16[8,128,128]{2,1,0:T(8,128)(2,1)S(1)}, u32[]{:S(2)}, u32[]{:S(2)}) collective-permute-start(bf16[8,128,128]{2,1,0:T(8,128)(2,1)S(1)} %all-to-all-done.refs_0_), channel_id=1, source_target_pairs={{0,16},{8,24},{16,0},{24,8},{1,17},{9,25},{17,1},{25,9},{2,18},{10... | collective-permute-start | bytes 786440 | tf_op jit(solution)/shard_map/ppermute | solution.py:399
  61.7 7.9 %copy-start.1 = (bf16[8,128,128]{2,1,0:T(8,128)(2,1)}, bf16[8,128,128]{2,1,0:T(8,128)(2,1)S(1)}, u32[]{:S(2)}) copy-start(bf16[8,128,128]{2,1,0:T(8,128)(2,1)S(1)} %all-to-all-done.1.refs_1_) | copy-start | bytes 786436
  61.7 6.4 %collective-permute-start.5 = (bf16[8,128,128]{2,1,0:T(8,128)(2,1)S(1)}, bf16[8,128,128]{2,1,0:T(8,128)(2,1)S(1)}, u32[]{:S(2)}, u32[]{:S(2)}) collective-permute-start(bf16[8,128,128]{2,1,0:T(8,128)(2,1)S(1)} %all-to-all-done.1.refs_1_), channel_id=1, source_target_pairs={{0,16},{8,24},{16,0},{24,8},{1,17},{9,25},{17,1},{25,9},{2,18},{10... | collective-permute-start | bytes 786440 | tf_op jit(solution)/shard_map/ppermute | solution.py:399
  63.2 4.9 %collective-permute-start.2 = (bf16[8,128,128]{2,1,0:T(8,128)(2,1)S(1)}, bf16[8,128,128]{2,1,0:T(8,128)(2,1)S(1)}, u32[]{:S(2)}, u32[]{:S(2)}) collective-permute-start(bf16[8,128,128]{2,1,0:T(8,128)(2,1)S(1)} %all-to-all-done.refs_0_), channel_id=1, source_target_pairs={{0,8},{8,0},{16,24},{24,16},{1,9},{9,1},{17,25},{25,17},{2,10},{10... | collective-permute-start | bytes 786440 | tf_op jit(solution)/shard_map/ppermute | solution.py:399
  63.2 4.9 %collective-permute-start.3 = (bf16[8,128,128]{2,1,0:T(8,128)(2,1)S(1)}, bf16[8,128,128]{2,1,0:T(8,128)(2,1)S(1)}, u32[]{:S(2)}, u32[]{:S(2)}) collective-permute-start(bf16[8,128,128]{2,1,0:T(8,128)(2,1)S(1)} %all-to-all-done.1.refs_1_), channel_id=1, source_target_pairs={{0,8},{8,0},{16,24},{24,16},{1,9},{9,1},{17,25},{25,17},{2,10},{10... | collective-permute-start | bytes 786440 | tf_op jit(solution)/shard_map/ppermute | solution.py:399
  63.7 5.9 %copy-start.4 = (bf16[8,128,128]{2,1,0:T(8,128)(2,1)}, bf16[8,128,128]{2,1,0:T(8,128)(2,1)S(1)}, u32[]{:S(2)}) copy-start(bf16[8,128,128]{2,1,0:T(8,128)(2,1)S(1)} %collective-permute-done.4.refs_4_) | copy-start | bytes 786436
  63.7 4.4 %collective-permute-start.6 = (bf16[8,128,128]{2,1,0:T(8,128)(2,1)S(1)}, bf16[8,128,128]{2,1,0:T(8,128)(2,1)S(1)}, u32[]{:S(2)}, u32[]{:S(2)}) collective-permute-start(bf16[8,128,128]{2,1,0:T(8,128)(2,1)S(1)} %collective-permute-done.4.refs_4_), channel_id=1, source_target_pairs={{0,8},{8,0},{16,24},{24,16},{1,9},{9,1},{17,25},{25,17},{2,10},{10... | collective-permute-start | bytes 786440 | tf_op jit(solution)/shard_map/ppermute | solution.py:399
  68.1 1.6 %copy-start.5 = (bf16[8,128,128]{2,1,0:T(8,128)(2,1)}, bf16[8,128,128]{2,1,0:T(8,128)(2,1)S(1)}, u32[]{:S(2)}) copy-start(bf16[8,128,128]{2,1,0:T(8,128)(2,1)S(1)} %collective-permute-done.5.refs_5_) | copy-start | bytes 786436
  68.1 1.5 %collective-permute-start.7 = (bf16[8,128,128]{2,1,0:T(8,128)(2,1)S(1)}, bf16[8,128,128]{2,1,0:T(8,128)(2,1)S(1)}, u32[]{:S(2)}, u32[]{:S(2)}) collective-permute-start(bf16[8,128,128]{2,1,0:T(8,128)(2,1)S(1)} %collective-permute-done.5.refs_5_), channel_id=1, source_target_pairs={{0,8},{8,0},{16,24},{24,16},{1,9},{9,1},{17,25},{25,17},{2,10},{10... | collective-permute-start | bytes 786440 | tf_op jit(solution)/shard_map/ppermute | solution.py:399
  68.1 1.6 %copy-start.6 = (bf16[8,128,128]{2,1,0:T(8,128)(2,1)}, bf16[8,128,128]{2,1,0:T(8,128)(2,1)S(1)}, u32[]{:S(2)}) copy-start(bf16[8,128,128]{2,1,0:T(8,128)(2,1)S(1)} %collective-permute-done.2.refs_2_) | copy-start | bytes 786436
  68.1 1.5 %copy-start.7 = (bf16[8,128,128]{2,1,0:T(8,128)(2,1)}, bf16[8,128,128]{2,1,0:T(8,128)(2,1)S(1)}, u32[]{:S(2)}) copy-start(bf16[8,128,128]{2,1,0:T(8,128)(2,1)S(1)} %collective-permute-done.3.refs_3_) | copy-start | bytes 786436
  68.2 1.5 %copy-start.8 = (bf16[8,128,128]{2,1,0:T(8,128)(2,1)}, bf16[8,128,128]{2,1,0:T(8,128)(2,1)S(1)}, u32[]{:S(2)}) copy-start(bf16[8,128,128]{2,1,0:T(8,128)(2,1)S(1)} %collective-permute-done.6.refs_6_) | copy-start | bytes 786436
  69.6 0.7 copy-start.9
